TPU v7x, 256 devices: a whole 4x4x8 slice. The times are simulated.
256 devices in a mesh: dp: 2 (over core), ctx: 16 (over y, x), tp: 8 (over z).
Axes of the slice: x: 4, y: 4, z: 8, core: 2. Of those that a mesh axis runs over, the one named last changes fastest.
Arguments:
- queries: bfloat16 [2, 2048, 8192], P('dp', 'ctx', 'tp'), may hold values from -160 to 160
- keys: bfloat16 [2, 2048, 512], P('dp', 'ctx'), may hold values from -6 to 6
- attention_values: bfloat16 [2, 2048, 512], P('dp', 'ctx'), may hold values from -6 to 6
- key_start: int32 [2, 2048], P('dp', 'ctx'), may hold values from 0 to 2040, as said below
- out_weight: bfloat16 [8192, 4096], P('tp', 'ctx'), may hold values from -0.29882812 to 0.29882812
- residual: bfloat16 [2, 2048, 4096], P('dp', ('ctx', 'tp')), may hold values from -40 to 40
- norm_gain: bfloat16 [4096], replicated, may hold values from 0.099609375 to 1.8984375
- router_weight: bfloat16 [4096, 128], replicated, may hold values from -0.015625 to 0.015625
- routes: int32 [2, 2048, 8], P('dp', ('ctx', 'tp')), may hold values from 0 to 127, all different within a row; in each aligned block of 16 rows (0 to 15, 16 to 31, ..., all dimensions but the last counted through in order) at most 2 rows name the same one
- block_masks: int32 [2, 2048, 8], P('dp', ('ctx', 'tp')), may hold values from 0 to 63
- gate_weight: bfloat16 [128, 4096, 768], P(('ctx', 'tp'), None, 'dp'), may hold values from -0.09375 to 0.09375
- up_weight: bfloat16 [128, 4096, 768], P(('ctx', 'tp'), None, 'dp'), may hold values from -0.09375 to 0.09375
- down_weight: bfloat16 [128, 768, 4096], P(('ctx', 'tp'), 'dp'), may hold values from -0.875 to 0.875
Outputs:
- layer_out: bfloat16 [2, 2048, 4096], P('dp', ('ctx', 'tp'))
Inputs may be any that keep to these rules, and one draw needn't show every extreme that they name: key_start[w, i] is the first position of token i's document in window w: a multiple of 8, at most i, equal for all tokens of a document; a window holds at most 4 documents. `routes`: each token names 8 different experts; among the rows of one device (aligned blocks of 16 tokens) no expert is named by more than 2 rows, a bound that some block reaches. `block_masks`: bit b keeps hidden units b * 128 up to (b + 1) * 128 - 1 of the route's expert.
All inputs are finite; a program needn't handle non-finite values.
Results may differ from a plain program's by a relative error of at most 0.017.
Values may be sent and summed in bfloat16 or wider, within the bound.
No kernel may reach another device: no remote copies, remote signals or barrier semaphores. Data moves between devices by JAX's collectives and lax.ppermute only.
A program may use at most 128 MiB of HBM per device.

v0:
```python
import math

import jax
import jax.numpy as jnp
from jax import lax
from jax.experimental import pallas as pl
from jax.experimental.pallas import tpu as pltpu
from jax.sharding import Mesh
from jax.sharding import PartitionSpec as P

QUERY_HEADS = 64
KEY_VALUE_HEADS = 4
HEAD_SIZE = 128
MASK_BLOCKS = 6
TOP = 8
EXPERTS = 128
CAP = 2
SCORE_FLOOR = -1e30
LANES = 128
SUB = 16
MIB = 1024 * 1024

CY, CX, ZHI, ZLO = 4, 4, 4, 2
CTX = ("cy", "cx")
F32, BF16, I32 = jnp.float32, jnp.bfloat16, jnp.int32


def call(kernel, out_shape, args, vmem, scalars=(), any_args=(), scratch=(), flops=0, moved=0):
    specs = [pl.BlockSpec(memory_space=pltpu.SMEM) for _ in scalars]
    specs += [pl.BlockSpec(memory_space=pltpu.VMEM) for _ in args]
    specs += [pl.BlockSpec(memory_space=pl.ANY) for _ in any_args]
    many = isinstance(out_shape, (list, tuple))
    whole = pl.BlockSpec(memory_space=pltpu.VMEM)
    return pl.pallas_call(
        kernel,
        out_shape=out_shape,
        in_specs=specs,
        out_specs=[whole] * len(out_shape) if many else whole,
        scratch_shapes=list(scratch),
        cost_estimate=pl.CostEstimate(flops=flops, bytes_accessed=moved, transcendentals=0),
        compiler_params=pltpu.CompilerParams(vmem_limit_bytes=vmem * MIB),
    )(*scalars, *args, *any_args)


def head_kernel(head_ref, key_ref, value_ref, out_ref, pair_ref, sems):
    columns = pl.ds(pl.multiple_of(head_ref[0] * HEAD_SIZE, HEAD_SIZE), HEAD_SIZE)
    copies = [
        pltpu.make_async_copy(ref.at[:, columns], pair_ref.at[i], sems.at[i])
        for i, ref in enumerate((key_ref, value_ref))
    ]
    for copy in copies:
        copy.start()
    for copy in copies:
        copy.wait()
    pair = jnp.concatenate([pair_ref[0], pair_ref[1]], axis=1)
    for c in range(out_ref.shape[0]):
        out_ref[c] = pair


def attend_kernel(first_ref, kv_ref, start_ref, query_hbm, out_ref, bias_ref, query_ref, sem):
    copy = pltpu.make_async_copy(query_hbm, query_ref, sem.at[0])
    copy.start()
    tokens = query_ref.shape[0]
    heads = query_ref.shape[1] // HEAD_SIZE
    keys = kv_ref.shape[0] * kv_ref.shape[1]
    key_rows = kv_ref[:, :, :HEAD_SIZE].reshape(keys, HEAD_SIZE)
    value_rows = kv_ref[:, :, HEAD_SIZE:].reshape(keys, HEAD_SIZE)
    position = first_ref[0] + lax.broadcasted_iota(I32, (tokens, keys), 0)
    key_pos = lax.broadcasted_iota(I32, (tokens, keys), 1)
    visible = (key_pos >= start_ref[...]) & (key_pos <= position)
    bias_ref[...] = jnp.where(visible, 0.0, SCORE_FLOOR)
    copy.wait()
    scale = math.log2(math.e) / math.sqrt(HEAD_SIZE)
    bias = bias_ref[...]
    bias = jnp.concatenate([bias, bias], axis=0)
    for head in range(0, heads, 2):
        columns = [slice(h * HEAD_SIZE, (h + 1) * HEAD_SIZE) for h in (head, head + 1)]
        scores = lax.dot_general(
            jnp.concatenate([query_ref[:, c] for c in columns], axis=0),
            key_rows,
            (((1,), (1,)), ((), ())),
            preferred_element_type=F32,
        )
        scores = scores * scale + bias
        row_max = jnp.max(scores, axis=1, keepdims=True)
        weights = jnp.exp2(scores - row_max)
        row_sum = jnp.sum(weights, axis=1, keepdims=True)
        mixed = jnp.dot(weights.astype(BF16), value_rows, preferred_element_type=F32)
        attended = (mixed / row_sum).astype(BF16)
        for which in range(2):
            for z in range(ZHI * ZLO):
                block = attended[which * tokens + z * SUB : which * tokens + (z + 1) * SUB]
                rows = slice((z // ZLO) * SUB, (z // ZLO + 1) * SUB)
                for y in range(CY):
                    out_ref[y * ZLO + z % ZLO, rows, columns[which]] = block


def project_kernel(dp_ref, x_ref, zlo_ref, att_ref, *refs):
    count = 2 * CX * ZLO
    sources, out_ref, held_ref, sems = refs[:count], refs[count], refs[count + 1], refs[count + 2]
    copies = [
        pltpu.make_async_copy(source, held_ref.at[i], sems.at[i]) for i, source in enumerate(sources)
    ]
    for copy in copies:
        copy.start()
    half, width = held_ref.shape[1:]
    rows = att_ref.shape[0] * att_ref.shape[2]
    for step, away in enumerate((0, CX - 1, 1, 2)):
        total = jnp.zeros((rows, width), F32)
        for part in range(2):
            columns = pl.ds(
                pl.multiple_of((dp_ref[0] if part == 0 else 1 - dp_ref[0]) * half, half), half
            )
            for near in range(ZLO):
                source = zlo_ref[0] if near == 0 else 1 - zlo_ref[0]
                piece = CX * ZLO * part + ZLO * step + near
                copies[piece].wait()
                total += jnp.dot(
                    att_ref[:, source, :, columns].reshape(rows, half),
                    held_ref[piece],
                    preferred_element_type=F32,
                )
        place = pl.multiple_of(((x_ref[0] + away) & (CX - 1)) * width, width)
        out_ref[:, :, pl.ds(place, width)] = total.astype(BF16).reshape(rows // SUB, SUB, width)


def norm_kernel(parts_ref, residual_ref, gain_ref, meta_ref, ext_ref, hidden_ref):
    model_width = residual_ref.shape[1]
    width = model_width // CY
    zs = ZHI
    pieces = []
    square_sum = jnp.zeros((SUB, 1), F32)
    for y in range(CY):
        columns = slice(y * width, (y + 1) * width)
        projected = sum(parts_ref[y * zs + z].astype(F32) for z in range(zs))
        hidden = (residual_ref[:, columns].astype(F32) + projected).astype(BF16)
        hidden_ref[:, columns] = hidden
        wide = hidden.astype(F32)
        square_sum += jnp.sum(wide * wide, axis=1, keepdims=True)
        pieces.append(wide)
    inverse = lax.rsqrt(square_sum / model_width + 1e-06)
    for y in range(CY):
        columns = slice(y * width, (y + 1) * width)
        normed = (pieces[y] * inverse * gain_ref[:, columns].astype(F32)).astype(BF16)
        ext_ref[:, columns] = normed
    ext_ref[:, model_width:] = meta_ref[...]


def slot_hits(meta, zhi, slots, slot_capacity):
    tokens = meta.shape[0]
    slot = lax.broadcasted_iota(I32, (tokens, slots), 1)
    dest = slot >> (slot_capacity.bit_length() - 1)
    expert = (dest >> 1) * (ZHI * ZLO) + zhi * ZLO + (dest & 1)
    hits = [meta[:, k : k + 1].astype(F32).astype(I32) == expert for k in range(TOP)]
    named = sum(h.astype(F32) for h in hits)
    later = lax.broadcasted_iota(I32, (tokens, tokens), 0) > lax.broadcasted_iota(
        I32, (tokens, tokens), 1
    )
    earlier = jnp.dot(later.astype(BF16), named.astype(BF16), preferred_element_type=F32)
    place = (slot & (slot_capacity - 1)).astype(F32)
    chosen = jnp.where((named > 0.5) & (earlier == place), 1.0, 0.0)
    return hits, chosen


def gathered_rows(refs):
    own, left, right, far_first, far_second = [ref[...] for ref in refs]
    far = jnp.concatenate([far_first, far_second], axis=1)
    return jnp.concatenate([own, left, right, far], axis=0)


def dispatch_kernel(zhi_ref, *refs):
    ext, rows_ref = gathered_rows(refs[:-1]), refs[-1]
    tokens = ext.shape[0]
    width = ext.shape[1] - LANES
    meta = ext[:, width:]
    hits, chosen = slot_hits(meta, zhi_ref[0], rows_ref.shape[0], tokens // SUB * CAP)
    masks = sum(
        jnp.where(hits[k], meta[:, TOP + k : TOP + k + 1].astype(F32), 0.0) for k in range(TOP)
    )
    along = (((0,), (0,)), ((), ()))
    rows_ref[:, :width] = lax.dot_general(
        chosen.astype(BF16), ext[:, :width], along, preferred_element_type=F32
    ).astype(BF16)
    ones = jnp.ones((tokens, LANES), BF16)
    rows_ref[:, width:] = lax.dot_general(
        (masks * chosen).astype(BF16), ones, along, preferred_element_type=F32
    ).astype(BF16)


def weight_kernel(zhi_ref, router_ref, *refs):
    ext, out_ref = gathered_rows(refs[:-1]), refs[-1]
    tokens = ext.shape[0]
    model_width = ext.shape[1] - LANES
    slots = out_ref.shape[1]
    meta, normed = ext[:, model_width:], ext[:, :model_width]
    logits = jnp.dot(normed, router_ref[...], preferred_element_type=F32)
    lanes = lax.broadcasted_iota(I32, (tokens, EXPERTS), 1)
    exps = []
    for k in range(TOP):
        route = meta[:, k : k + 1].astype(F32).astype(I32)
        picked = jnp.sum(jnp.where(lanes == route, logits, 0.0), axis=1, keepdims=True)
        exps.append(jnp.exp(picked))
    total = sum(exps)
    hits, chosen = slot_hits(meta, zhi_ref[0], slots, tokens // SUB * CAP)
    route_weight = sum(jnp.where(hits[k], exps[k] / total, 0.0) for k in range(TOP))
    out_ref[...] = route_weight * chosen


def expert_kernel(dp_ref, rows_ref, *refs):
    weights, out_ref, held, sems = refs[:6], refs[6], refs[7:13], refs[13]
    copies = [pltpu.make_async_copy(weights[i], held[i], sems.at[i]) for i in range(6)]
    for i in (0, 1, 3, 4, 2, 5):
        copies[i].start()
    model_width = out_ref.shape[1]
    masks = rows_ref[:, model_width:].astype(F32).astype(I32)
    blocks = MASK_BLOCKS // 2
    acts = []
    for part in range(2):
        gate_ref, up_ref = held[3 * part], held[3 * part + 1]
        first = (dp_ref[0] if part == 0 else 1 - dp_ref[0]) * blocks
        copies[3 * part].wait()
        copies[3 * part + 1].wait()
        both = jnp.dot(
            rows_ref[:, :model_width],
            jnp.concatenate([gate_ref[...], up_ref[...]], axis=1),
            preferred_element_type=F32,
        )
        units = gate_ref.shape[1]
        keep = jnp.concatenate(
            [(jnp.right_shift(masks, first + b) & 1).astype(F32) for b in range(blocks)], axis=1
        )
        acts.append((jax.nn.silu(both[:, :units]) * both[:, units:] * keep).astype(BF16))
    copies[2].wait()
    copies[5].wait()
    activated = jnp.concatenate(acts, axis=1)
    step = 512
    for j in range(model_width // step):
        columns = slice(j * step, (j + 1) * step)
        down = jnp.concatenate([held[2][:, columns], held[5][:, columns]], axis=0)
        out_ref[:, columns] = jnp.dot(activated, down, preferred_element_type=F32).astype(BF16)


def combine_kernel(zhi_ref, weight_ref, back_ref, out_ref):
    weight = weight_ref[...]
    high = weight.astype(BF16)
    rest = weight - high.astype(F32)
    middle = rest.astype(BF16)
    low = (rest - middle.astype(F32)).astype(BF16)
    stacked = jnp.concatenate([high, middle, low], axis=0)
    tokens = weight.shape[0]
    model_width = back_ref.shape[1]
    step = 1024
    for j in range(model_width // step):
        columns = slice(j * step, (j + 1) * step)
        parts = jnp.dot(stacked, back_ref[:, columns], preferred_element_type=F32)
        total = parts[:tokens] + parts[tokens : 2 * tokens] + parts[2 * tokens :]
        total = total.astype(BF16)
        for place, away in enumerate((0, ZHI - 1, 1, 2)):
            home = (zhi_ref[0] + away) & (ZHI - 1)
            out_ref[home, :, columns] = total[place * SUB : (place + 1) * SUB]


def stay(x):
    return pltpu.with_memory_space_constraint(x, pltpu.HBM)


def swap(n):
    return [(i, i ^ 1) for i in range(n)]


def ring(n, step):
    return [(i, (i + step) % n) for i in range(n)]


def exchange(x, axes):
    return lax.all_to_all(x, axes, split_axis=0, concat_axis=0, tiled=True)


def local(
    queries,
    keys,
    attention_values,
    key_start,
    out_weight,
    residual,
    norm_gain,
    router_weight,
    routes,
    block_masks,
    gate_weight,
    up_weight,
    down_weight,
):
    dp = lax.axis_index("dp").astype(I32)
    ctx = lax.axis_index(CTX).astype(I32)
    zhi, zlo = lax.axis_index("zhi").astype(I32), lax.axis_index("zlo").astype(I32)
    tokens = queries.shape[1]
    model_width = residual.shape[2]
    token_rows = residual.shape[1]
    ctx_count = CY * CX
    scalar = lambda v: v.reshape(1)

    with jax.named_scope("keys_values"):
        heads = queries.shape[2] // HEAD_SIZE
        kv_head = (zhi * ZLO + zlo) * heads // (QUERY_HEADS // KEY_VALUE_HEADS)
        copies = call(
            head_kernel,
            jax.ShapeDtypeStruct((ctx_count, tokens, 2 * HEAD_SIZE), BF16),
            (),
            vmem=8,
            scalars=(scalar(kv_head),),
            any_args=(stay(keys[0]), stay(attention_values[0])),
            scratch=[pltpu.VMEM((2, tokens, HEAD_SIZE), BF16), pltpu.SemaphoreType.DMA((2,))],
            moved=2 << 20,
        )
        all_kv = exchange(copies, CTX)

    with jax.named_scope("expert_weights"):
        own_experts = [a[0] for a in (gate_weight, up_weight, down_weight)]
        other_experts = [lax.ppermute(a, "dp", swap(2)) for a in own_experts]

    with jax.named_scope("out_weight"):
        half = out_weight.shape[0] // 2
        own_half = lax.dynamic_slice_in_dim(out_weight, dp * half, half, 0)
        beside = lax.ppermute(own_half, "zlo", swap(ZLO))
        own_other = lax.ppermute(own_half, "dp", swap(2))
        all_kv, beside, own_other, other_experts = lax.optimization_barrier(
            (all_kv, beside, own_other, other_experts)
        )
        left_own = lax.ppermute(own_half, "cx", ring(CX, 1))
        right_beside = lax.ppermute(beside, "cx", ring(CX, -1))
        left_beside = lax.ppermute(beside, "cx", ring(CX, 1))
        right_own = lax.ppermute(own_half, "cx", ring(CX, -1))
        beside_other = lax.ppermute(beside, "dp", swap(2))

    with jax.named_scope("attention"):
        attended = call(
            attend_kernel,
            jax.ShapeDtypeStruct((CY * ZLO, tokens // ZLO, queries.shape[2]), BF16),
            (all_kv, key_start.reshape(tokens, 1)),
            vmem=28,
            scalars=(scalar(ctx * tokens),),
            any_args=(stay(queries[0]),),
            scratch=[
                pltpu.VMEM((tokens, ctx_count * tokens), F32),
                pltpu.VMEM((tokens, queries.shape[2]), BF16),
                pltpu.SemaphoreType.DMA((1,)),
            ],
            flops=4 * tokens * heads * ctx_count * tokens * HEAD_SIZE,
            moved=4 << 20,
        )
        attended, left_own, left_beside, right_own, right_beside, beside_other = (
            lax.optimization_barrier(
                (attended, left_own, left_beside, right_own, right_beside, beside_other)
            )
        )
        far_own = lax.ppermute(left_own, "cx", ring(CX, 1))
        far_beside = lax.ppermute(right_beside, "cx", ring(CX, -1))
        near = [own_half, beside]
        later = [left_own, left_beside, right_own, right_beside, far_own, far_beside]
        others = [own_other, beside_other] + [lax.ppermute(w, "dp", swap(2)) for w in later]
        gathered = exchange(attended, ("cy", "zlo"))
        gathered = gathered.reshape(CY, ZLO, tokens // ZLO, queries.shape[2])

    with jax.named_scope("projection"):
        half, width = out_weight.shape[0] // 2, out_weight.shape[1]
        group_rows = CY * ZHI * token_rows
        mine, x = scalar(dp), scalar(lax.axis_index("cx").astype(I32))
        partial = call(
            project_kernel,
            jax.ShapeDtypeStruct((CY * ZHI, SUB, model_width // CY), BF16),
            (gathered,),
            vmem=14,
            scalars=(mine, x, scalar(zlo)),
            any_args=[stay(w) for w in near + later + others[:2]] + others[2:],
            scratch=[
                pltpu.VMEM((2 * CX * ZLO, half, width), BF16),
                pltpu.SemaphoreType.DMA((2 * CX * ZLO,)),
            ],
            flops=2 * group_rows * 16 * half * width,
            moved=6 << 20,
        )
        parts = exchange(partial, ("cy", "zhi"))

    with jax.named_scope("norm"):
        meta = jnp.concatenate([routes[0], block_masks[0]], axis=1).astype(BF16)
        meta = jnp.pad(meta, ((0, 0), (0, LANES - 2 * TOP)))
        ext, hidden_state = call(
            norm_kernel,
            [
                jax.ShapeDtypeStruct((token_rows, model_width + LANES), BF16),
                jax.ShapeDtypeStruct((token_rows, model_width), BF16),
            ],
            (parts, residual[0], norm_gain.reshape(1, model_width), meta),
            vmem=6,
            moved=2 << 20,
        )
        left = lax.ppermute(ext, "zhi", ring(ZHI, 1))
        right = lax.ppermute(ext, "zhi", ring(ZHI, -1))
        cut = model_width // 2
        far = [
            lax.ppermute(left[:, :cut], "zhi", ring(ZHI, 1)),
            lax.ppermute(right[:, cut:], "zhi", ring(ZHI, -1)),
        ]
        near_ext = (ext, left, right, *far)

    with jax.named_scope("dispatch"):
        dests = ctx_count * ZLO
        capacity = ZHI * token_rows // SUB * CAP
        slots = dests * capacity
        rows = call(
            dispatch_kernel,
            jax.ShapeDtypeStruct((slots, model_width + LANES), BF16),
            near_ext,
            vmem=16,
            scalars=(scalar(zhi),),
            flops=2 * slots * 64 * model_width,
            moved=3 << 20,
        )
        slot_weight = call(
            weight_kernel,
            jax.ShapeDtypeStruct((ZHI * token_rows, slots), F32),
            (router_weight, *near_ext),
            vmem=8,
            scalars=(scalar(zhi),),
            flops=2 * 64 * EXPERTS * model_width,
            moved=2 << 20,
        )
        over = ("cy", "cx", "zlo")
        got = exchange(rows.reshape(dests, capacity, model_width + LANES), over)

    with jax.named_scope("experts"):
        every = own_experts + other_experts
        expert_out = call(
            expert_kernel,
            jax.ShapeDtypeStruct((slots, model_width), BF16),
            (got.reshape(slots, model_width + LANES),),
            vmem=32,
            scalars=(scalar(dp),),
            any_args=[stay(w) if i % 3 == 2 else w for i, w in enumerate(every)],
            scratch=[pltpu.VMEM(a.shape, a.dtype) for a in every] + [pltpu.SemaphoreType.DMA((6,))],
            flops=6 * slots * model_width * 768,
            moved=22 << 20,
        )
        back = exchange(expert_out.reshape(dests, capacity, model_width), over)

    with jax.named_scope("combine"):
        mixed = call(
            combine_kernel,
            jax.ShapeDtypeStruct((ZHI, token_rows, model_width), BF16),
            (slot_weight, back.reshape(slots, model_width)),
            vmem=14,
            scalars=(scalar(zhi),),
            flops=6 * 64 * slots * model_width,
            moved=3 << 20,
        )
        mixture = jnp.sum(exchange(mixed, "zhi").astype(F32), axis=0)
        layer_out = (hidden_state.astype(F32) + mixture).astype(BF16)
    return layer_out[None]


def solution(mesh):
    fine = Mesh(
        mesh.devices.reshape(2, CY, CX, ZHI, ZLO), ("dp", "cy", "cx", "zhi", "zlo")
    )
    tp = ("zhi", "zlo")
    all_ctx = CTX + tp
    in_specs = (
        P("dp", CTX, tp),
        P("dp", CTX, None),
        P("dp", CTX, None),
        P("dp", CTX),
        P(tp, CTX),
        P("dp", all_ctx, None),
        P(),
        P(),
        P("dp", all_ctx, None),
        P("dp", all_ctx, None),
        P(all_ctx, None, "dp"),
        P(all_ctx, None, "dp"),
        P(all_ctx, "dp", None),
    )
    out_specs = P("dp", all_ctx, None)
    return jax.shard_map(local, mesh=fine, in_specs=in_specs, out_specs=out_specs, check_vma=False)
```

profile of v0, /device:TPU:32, one launch (start us, length us, event | category | flops | bytes accessed | tf_op | source)
XLA Modules:
  0.0 199.3 jit_solution(13468598812867216747)
XLA Ops:
  0.6 1.9 keys_values.1
  2.5 7.0 %all-to-all-start = ((bf16[16,128,256]{2,1,0:T(8,128)(2,1)}), bf16[16,128,256]{2,1,0:T(8,128)(2,1)S(1)}, u32[]{:S(2)}, u32[]{:S(2)}) async-start(bf16[16,128,256]{2,1,0:T(8,128)(2,1)} %keys_values.1), calls=%async_computation | async-start | bytes 2097152 | tf_op jit(solution)/shard_map/keys_values/all_to_all | solution.py:276
  9.9 8.1 %collective-permute-done.refs_1_ = bf16[512,256]{1,0:T(8,128)(2,1)S(1)} collective-permute-done((bf16[512,256]{1,0:T(8,128)(2,1)S(1)}, bf16[512,256]{1,0:T(8,128)(2,1)S(1)}, u32[]{:S(2)}, u32[]{:S(2)}) %collective-permute-start) | collective-permute-done | bytes 262176 | tf_op jit(solution)/shard_map/out_weight/ppermute | solution.py:325
  18.1 1.6 collective-permute-start.5
  19.7 1.6 collective-permute-start.7
  21.3 7.4 %all-to-all-done.kv_ref = bf16[16,128,256]{2,1,0:T(8,128)(2,1)S(1)} async-done(((bf16[16,128,256]{2,1,0:T(8,128)(2,1)}), bf16[16,128,256]{2,1,0:T(8,128)(2,1)S(1)}, u32[]{:S(2)}, u32[]{:S(2)}) %all-to-all-start) | async-done | bytes 1048608 | tf_op jit(solution)/shard_map/keys_values/all_to_all | solution.py:276
  28.8 3.2 %collective-permute-start.8 = (bf16[512,256]{1,0:T(8,128)(2,1)S(1)}, bf16[512,256]{1,0:T(8,128)(2,1)}, u32[]{:S(2)}, u32[]{:S(2)}) collective-permute-start(bf16[512,256]{1,0:T(8,128)(2,1)S(1)} %collective-permute-done.refs_1_), channel_id=1, source_target_pairs={{0,24},{8,0},{16,8},{24,16},{1,25},{9,1},{17,9},{25,17},{2,26},{10... | collective-permute-start | bytes 786440 | tf_op jit(solution)/shard_map/out_weight/ppermute | solution.py:331
  32.1 5.7 %attention.1 = bf16[8,64,1024]{2,1,0:T(8,128)(2,1)} custom-call(s32[1]{0:T(128)} %bitcast.3.first_ref, bf16[16,128,256]{2,1,0:T(8,128)(2,1)S(1)} %all-to-all-done.kv_ref, s32[128,1]{1,0:T(8,128)S(1)} %copy.14.start_ref, bf16[128,1024]{1,0:T(8,128)(2,1)} %bitcast.39), custom_call_target="tpu_custom_call" | custom-call | flops 1073741824 | bytes 4194304 | tf_op jit(solution)/shard_map/attention/pallas_call | solution.py:34
  37.9 4.0 %all-to-all-start.1 = ((bf16[8,64,1024]{2,1,0:T(8,128)(2,1)}), bf16[8,64,1024]{2,1,0:T(8,128)(2,1)S(1)}, u32[]{:S(2)}, u32[]{:S(2)}) async-start(bf16[8,64,1024]{2,1,0:T(8,128)(2,1)} %attention.1), calls=%async_computation.1 | async-start | bytes 2097152 | tf_op jit(solution)/shard_map/attention/all_to_all | solution.py:276
  42.2 3.0 %collective-permute-start.11 = (bf16[512,256]{1,0:T(8,128)(2,1)}, bf16[512,256]{1,0:T(8,128)(2,1)S(1)}, u32[]{:S(2)}, u32[]{:S(2)}) collective-permute-start(bf16[512,256]{1,0:T(8,128)(2,1)} %collective-permute-done.8.refs_5_), channel_id=1, source_target_pairs={{0,24},{8,0},{16,8},{24,16},{1,25},{9,1},{17,9},{25,17},{2,26},{10... | collective-permute-start | bytes 786440 | tf_op jit(solution)/shard_map/attention/ppermute | solution.py:358
  45.8 5.6 %collective-permute-done.10.refs_6_ = bf16[512,256]{1,0:T(8,128)(2,1)S(1)} collective-permute-done((bf16[512,256]{1,0:T(8,128)(2,1)S(1)}, bf16[512,256]{1,0:T(8,128)(2,1)S(1)}, u32[]{:S(2)}, u32[]{:S(2)}) %collective-permute-start.10) | collective-permute-done | bytes 262176 | tf_op jit(solution)/shard_map/attention/ppermute | solution.py:357
  53.7 3.3 %all-to-all-done.1 = bf16[8,64,1024]{2,1,0:T(8,128)(2,1)S(1)} async-done(((bf16[8,64,1024]{2,1,0:T(8,128)(2,1)}), bf16[8,64,1024]{2,1,0:T(8,128)(2,1)S(1)}, u32[]{:S(2)}, u32[]{:S(2)}) %all-to-all-start.1) | async-done | bytes 1048608 | tf_op jit(solution)/shard_map/attention/all_to_all | solution.py:276
  57.0 5.5 %projection.1 = bf16[16,16,1024]{2,1,0:T(8,128)(2,1)} custom-call(s32[1]{0:T(128)} %bitcast.dp_ref, s32[1]{0:T(128)} %bitcast.1.x_ref, s32[1]{0:T(128)} %bitcast.2.zlo_ref, bf16[4,2,64,1024]{3,2,1,0:T(8,128)(2,1)S(1)} %bitcast.28, bf16[512,256]{1,0:T(8,128)(2,1)} %copy-done.5, bf16[512,256]{1,0:T(8,128)(2,1)} %copy-done.6, bf16[512,256]{1,0:T(8,128)(2,1)} %copy-done.8, ...), custom_call_target="tpu_custom_call" | custom-call | flops 1073741824 | bytes 6291456 | tf_op jit(solution)/shard_map/projection/pallas_call | solution.py:34
  62.5 9.2 %all-to-all-start.2 = ((bf16[16,16,1024]{2,1,0:T(8,128)(2,1)}), bf16[16,16,1024]{2,1,0:T(8,128)(2,1)S(1)}, u32[]{:S(2)}, u32[]{:S(2)}) async-start(bf16[16,16,1024]{2,1,0:T(8,128)(2,1)} %projection.1), calls=%async_computation.2 | async-start | bytes 1048576 | tf_op jit(solution)/shard_map/projection/all_to_all | solution.py:276
  72.0 17.4 %all-to-all-done.2.parts_ref = bf16[16,16,1024]{2,1,0:T(8,128)(2,1)S(1)} async-done(((bf16[16,16,1024]{2,1,0:T(8,128)(2,1)}), bf16[16,16,1024]{2,1,0:T(8,128)(2,1)S(1)}, u32[]{:S(2)}, u32[]{:S(2)}) %all-to-all-start.2) | async-done | bytes 524320 | tf_op jit(solution)/shard_map/projection/all_to_all | solution.py:276
  89.9 2.7 %collective-permute-start.18 = (bf16[16,4224]{1,0:T(8,128)(2,1)S(1)}, bf16[16,4224]{1,0:T(8,128)(2,1)S(1)}, u32[]{:S(2)}, u32[]{:S(2)}) collective-permute-start(bf16[16,4224]{1,0:T(8,128)(2,1)S(1)} %get-tuple-element.29.refs_0_), channel_id=1, source_target_pairs={{0,2},{2,4},{4,6},{6,0},{1,3},{3,5},{5,7},{7,1},{8,10},{10,12},{12... | collective-permute-start | bytes 405512 | tf_op jit(solution)/shard_map/norm/ppermute | solution.py:398
  92.6 4.1 %collective-permute-done.19.refs_2_ = bf16[16,4224]{1,0:T(8,128)(2,1)S(1)} collective-permute-done((bf16[16,4224]{1,0:T(8,128)(2,1)S(1)}, bf16[16,4224]{1,0:T(8,128)(2,1)S(1)}, u32[]{:S(2)}, u32[]{:S(2)}) %collective-permute-start.19) | collective-permute-done | bytes 135200 | tf_op jit(solution)/shard_map/norm/ppermute | solution.py:399
  97.5 3.6 %collective-permute-start.20 = (bf16[16,2048]{1,0:T(8,128)(2,1)S(1)}, bf16[16,2048]{1,0:T(8,128)(2,1)S(1)}, u32[]{:S(2)}, u32[]{:S(2)}) collective-permute-start(bf16[16,2048]{1,0:T(8,128)(2,1)S(1)} %slice.8), channel_id=1, source_target_pairs={{0,2},{2,4},{4,6},{6,0},{1,3},{3,5},{5,7},{7,1},{8,10},{10,12},{12... | collective-permute-start | bytes 196616 | tf_op jit(solution)/shard_map/norm/ppermute | solution.py:402
  101.1 3.4 %collective-permute-done.20.refs_3_ = bf16[16,2048]{1,0:T(8,128)(2,1)S(1)} collective-permute-done((bf16[16,2048]{1,0:T(8,128)(2,1)S(1)}, bf16[16,2048]{1,0:T(8,128)(2,1)S(1)}, u32[]{:S(2)}, u32[]{:S(2)}) %collective-permute-start.20) | collective-permute-done | bytes 65568 | tf_op jit(solution)/shard_map/norm/ppermute | solution.py:402
  105.5 34.9 %all_to_all.30 = bf16[32,8,4224]{2,1,0:T(8,128)(2,1)S(1)} all-to-all(bf16[32,8,4224]{2,1,0:T(8,128)(2,1)S(1)} %bitcast.26), channel_id=1, replica_groups=mesh['dp'=2,'cy'=4,'cx'=4,'zhi'=4,'zlo'=2] {'cy','cx','zlo'}, dimensions={0} | all-to-all | bytes 4325376 | tf_op jit(solution)/shard_map/dispatch/all_to_all | solution.py:276
  140.5 8.8 %experts.1 = bf16[256,4096]{1,0:T(8,128)(2,1)} custom-call(s32[1]{0:T(128)} %bitcast.dp_ref, bf16[256,4224]{1,0:T(8,128)(2,1)S(1)} %bitcast.25, bf16[4096,384]{1,0:T(8,128)(2,1)S(1)} %bitcast.30, bf16[4096,384]{1,0:T(8,128)(2,1)S(1)} %bitcast.32, bf16[384,4096]{1,0:T(8,128)(2,1)} %bitcast.35, bf16[4096,384]{1,0:T(8,128)(2,1)} %collective-permute-done.2.refs_3_, ...), custom_call_target="tpu_custom_call" | custom-call | flops 4831838208 | bytes 23068672 | tf_op jit(solution)/shard_map/experts/pallas_call | solution.py:34
  149.3 5.0 %all-to-all-start.4 = ((bf16[32,8,4096]{2,1,0:T(8,128)(2,1)}), bf16[32,8,4096]{2,1,0:T(8,128)(2,1)S(1)}, u32[]{:S(2)}, u32[]{:S(2)}) async-start(bf16[32,8,4096]{2,1,0:T(8,128)(2,1)} %bitcast.19), calls=%async_computation.4 | async-start | bytes 4194304 | tf_op jit(solution)/shard_map/experts/all_to_all | solution.py:276
  156.1 24.4 %all-to-all-done.4 = bf16[32,8,4096]{2,1,0:T(8,128)(2,1)S(1)} async-done(((bf16[32,8,4096]{2,1,0:T(8,128)(2,1)}), bf16[32,8,4096]{2,1,0:T(8,128)(2,1)S(1)}, u32[]{:S(2)}, u32[]{:S(2)}) %all-to-all-start.4) | async-done | bytes 2097184 | tf_op jit(solution)/shard_map/experts/all_to_all | solution.py:276
  181.1 17.4 %all_to_all.31 = bf16[4,16,4096]{2,1,0:T(8,128)(2,1)S(1)} all-to-all(bf16[4,16,4096]{2,1,0:T(8,128)(2,1)S(1)} %combine.1), channel_id=1, replica_groups=mesh['dp'=2,'cy'=4,'cx'=4,'zhi'=4,'zlo'=2] {'zhi'}, dimensions={0} | all-to-all | bytes 1048576 | tf_op jit(solution)/shard_map/combine/all_to_all | solution.py:276
  (82 shorter events, 10.1 us)
Async XLA Ops:
  0.0 28.7 %collective-permute-start.2 = (bf16[4096,384]{1,0:T(8,128)(2,1)}, bf16[4096,384]{1,0:T(8,128)(2,1)}, u32[]{:S(2)}, u32[]{:S(2)}) collective-permute-start(bf16[4096,384]{1,0:T(8,128)(2,1)} %bitcast.29), channel_id=1, source_target_pairs={{0,128},{128,0},{1,129},{129,1},{2,130},{130,2},{3,131},{131,3},{4... | collective-permute-start | bytes 9437192 | tf_op jit(solution)/shard_map/expert_weights/ppermute | solution.py:320
  0.0 28.7 %collective-permute-start.3 = (bf16[4096,384]{1,0:T(8,128)(2,1)}, bf16[4096,384]{1,0:T(8,128)(2,1)}, u32[]{:S(2)}, u32[]{:S(2)}) collective-permute-start(bf16[4096,384]{1,0:T(8,128)(2,1)} %bitcast.31), channel_id=1, source_target_pairs={{0,128},{128,0},{1,129},{129,1},{2,130},{130,2},{3,131},{131,3},{4... | collective-permute-start | bytes 9437192 | tf_op jit(solution)/shard_map/expert_weights/ppermute | solution.py:320
  0.5 28.2 %collective-permute-start.4 = (bf16[384,4096]{1,0:T(8,128)(2,1)}, bf16[384,4096]{1,0:T(8,128)(2,1)}, u32[]{:S(2)}, u32[]{:S(2)}) collective-permute-start(bf16[384,4096]{1,0:T(8,128)(2,1)} %bitcast.34), channel_id=1, source_target_pairs={{0,128},{128,0},{1,129},{129,1},{2,130},{130,2},{3,131},{131,3},{4... | collective-permute-start | bytes 9437192 | tf_op jit(solution)/shard_map/expert_weights/ppermute | solution.py:320
  2.5 26.2 %all-to-all-start = ((bf16[16,128,256]{2,1,0:T(8,128)(2,1)}), bf16[16,128,256]{2,1,0:T(8,128)(2,1)S(1)}, u32[]{:S(2)}, u32[]{:S(2)}) async-start(bf16[16,128,256]{2,1,0:T(8,128)(2,1)} %keys_values.1), calls=%async_computation | async-start | bytes 2097152 | tf_op jit(solution)/shard_map/keys_values/all_to_all | solution.py:276
  9.6 8.4 %collective-permute-start = (bf16[512,256]{1,0:T(8,128)(2,1)S(1)}, bf16[512,256]{1,0:T(8,128)(2,1)S(1)}, u32[]{:S(2)}, u32[]{:S(2)}) collective-permute-start(bf16[512,256]{1,0:T(8,128)(2,1)S(1)} %constant_dynamic-slice_fusion.refs_0_), channel_id=1, source_target_pairs={{0,1},{1,0},{2,3},{3,2},{4,5},{5,4},{6,7},{7,6},{8,9},{9,8},{10,11... | collective-permute-start | bytes 786440 | tf_op jit(solution)/shard_map/out_weight/ppermute | solution.py:325
  9.8 9.9 %collective-permute-start.1 = (bf16[512,256]{1,0:T(8,128)(2,1)S(1)}, bf16[512,256]{1,0:T(8,128)(2,1)S(1)}, u32[]{:S(2)}, u32[]{:S(2)}) collective-permute-start(bf16[512,256]{1,0:T(8,128)(2,1)S(1)} %constant_dynamic-slice_fusion.refs_0_), channel_id=1, source_target_pairs={{0,128},{128,0},{1,129},{129,1},{2,130},{130,2},{3,131},{131,3},{4... | collective-permute-start | bytes 786440 | tf_op jit(solution)/shard_map/out_weight/ppermute | solution.py:326
  18.1 19.7 %collective-permute-start.5 = (bf16[512,256]{1,0:T(8,128)(2,1)S(1)}, bf16[512,256]{1,0:T(8,128)(2,1)S(1)}, u32[]{:S(2)}, u32[]{:S(2)}) collective-permute-start(bf16[512,256]{1,0:T(8,128)(2,1)S(1)} %constant_dynamic-slice_fusion.refs_0_), channel_id=1, source_target_pairs={{0,8},{8,16},{16,24},{24,0},{1,9},{9,17},{17,25},{25,1},{2,10},{10... | collective-permute-start | bytes 786440 | tf_op jit(solution)/shard_map/out_weight/ppermute | solution.py:330
  19.7 18.1 %collective-permute-start.7 = (bf16[512,256]{1,0:T(8,128)(2,1)S(1)}, bf16[512,256]{1,0:T(8,128)(2,1)}, u32[]{:S(2)}, u32[]{:S(2)}) collective-permute-start(bf16[512,256]{1,0:T(8,128)(2,1)S(1)} %constant_dynamic-slice_fusion.refs_0_), channel_id=1, source_target_pairs={{0,24},{8,0},{16,8},{24,16},{1,25},{9,1},{17,9},{25,17},{2,26},{10... | collective-permute-start | bytes 786440 | tf_op jit(solution)/shard_map/out_weight/ppermute | solution.py:333
  28.7 9.1 %collective-permute-start.6 = (bf16[512,256]{1,0:T(8,128)(2,1)S(1)}, bf16[512,256]{1,0:T(8,128)(2,1)}, u32[]{:S(2)}, u32[]{:S(2)}) collective-permute-start(bf16[512,256]{1,0:T(8,128)(2,1)S(1)} %collective-permute-done.refs_1_), channel_id=1, source_target_pairs={{0,8},{8,16},{16,24},{24,0},{1,9},{9,17},{17,25},{25,1},{2,10},{10... | collective-permute-start | bytes 786440 | tf_op jit(solution)/shard_map/out_weight/ppermute | solution.py:332
  28.8 9.0 %collective-permute-start.8 = (bf16[512,256]{1,0:T(8,128)(2,1)S(1)}, bf16[512,256]{1,0:T(8,128)(2,1)}, u32[]{:S(2)}, u32[]{:S(2)}) collective-permute-start(bf16[512,256]{1,0:T(8,128)(2,1)S(1)} %collective-permute-done.refs_1_), channel_id=1, source_target_pairs={{0,24},{8,0},{16,8},{24,16},{1,25},{9,1},{17,9},{25,17},{2,26},{10... | collective-permute-start | bytes 786440 | tf_op jit(solution)/shard_map/out_weight/ppermute | solution.py:331
  32.0 5.8 %collective-permute-start.9 = (bf16[512,256]{1,0:T(8,128)(2,1)S(1)}, bf16[512,256]{1,0:T(8,128)(2,1)S(1)}, u32[]{:S(2)}, u32[]{:S(2)}) collective-permute-start(bf16[512,256]{1,0:T(8,128)(2,1)S(1)} %collective-permute-done.refs_1_), channel_id=1, source_target_pairs={{0,128},{128,0},{1,129},{129,1},{2,130},{130,2},{3,131},{131,3},{4... | collective-permute-start | bytes 786440 | tf_op jit(solution)/shard_map/out_weight/ppermute | solution.py:334
  37.9 19.1 %all-to-all-start.1 = ((bf16[8,64,1024]{2,1,0:T(8,128)(2,1)}), bf16[8,64,1024]{2,1,0:T(8,128)(2,1)S(1)}, u32[]{:S(2)}, u32[]{:S(2)}) async-start(bf16[8,64,1024]{2,1,0:T(8,128)(2,1)} %attention.1), calls=%async_computation.1 | async-start | bytes 2097152 | tf_op jit(solution)/shard_map/attention/all_to_all | solution.py:276
  41.9 9.5 %collective-permute-start.10 = (bf16[512,256]{1,0:T(8,128)(2,1)S(1)}, bf16[512,256]{1,0:T(8,128)(2,1)S(1)}, u32[]{:S(2)}, u32[]{:S(2)}) collective-permute-start(bf16[512,256]{1,0:T(8,128)(2,1)S(1)} %collective-permute-done.5.refs_2_), channel_id=1, source_target_pairs={{0,8},{8,16},{16,24},{24,0},{1,9},{9,17},{17,25},{25,1},{2,10},{10... | collective-permute-start | bytes 786440 | tf_op jit(solution)/shard_map/attention/ppermute | solution.py:357
  42.2 9.3 %collective-permute-start.11 = (bf16[512,256]{1,0:T(8,128)(2,1)}, bf16[512,256]{1,0:T(8,128)(2,1)S(1)}, u32[]{:S(2)}, u32[]{:S(2)}) collective-permute-start(bf16[512,256]{1,0:T(8,128)(2,1)} %collective-permute-done.8.refs_5_), channel_id=1, source_target_pairs={{0,24},{8,0},{16,8},{24,16},{1,25},{9,1},{17,9},{25,17},{2,26},{10... | collective-permute-start | bytes 786440 | tf_op jit(solution)/shard_map/attention/ppermute | solution.py:358
  45.2 6.8 %collective-permute-start.12 = (bf16[512,256]{1,0:T(8,128)(2,1)S(1)}, bf16[512,256]{1,0:T(8,128)(2,1)S(1)}, u32[]{:S(2)}, u32[]{:S(2)}) collective-permute-start(bf16[512,256]{1,0:T(8,128)(2,1)S(1)} %collective-permute-done.5.refs_2_), channel_id=1, source_target_pairs={{0,128},{128,0},{1,129},{129,1},{2,130},{130,2},{3,131},{131,3},{4... | collective-permute-start | bytes 786440 | tf_op jit(solution)/shard_map/attention/ppermute | solution.py:361
  45.2 8.0 %collective-permute-start.15 = (bf16[512,256]{1,0:T(8,128)(2,1)}, bf16[512,256]{1,0:T(8,128)(2,1)S(1)}, u32[]{:S(2)}, u32[]{:S(2)}) collective-permute-start(bf16[512,256]{1,0:T(8,128)(2,1)} %collective-permute-done.8.refs_5_), channel_id=1, source_target_pairs={{0,128},{128,0},{1,129},{129,1},{2,130},{130,2},{3,131},{131,3},{4... | collective-permute-start | bytes 786440 | tf_op jit(solution)/shard_map/attention/ppermute | solution.py:361
  45.7 6.4 %collective-permute-start.13 = (bf16[512,256]{1,0:T(8,128)(2,1)}, bf16[512,256]{1,0:T(8,128)(2,1)S(1)}, u32[]{:S(2)}, u32[]{:S(2)}) collective-permute-start(bf16[512,256]{1,0:T(8,128)(2,1)} %collective-permute-done.6.refs_3_), channel_id=1, source_target_pairs={{0,128},{128,0},{1,129},{129,1},{2,130},{130,2},{3,131},{131,3},{4... | collective-permute-start | bytes 786440 | tf_op jit(solution)/shard_map/attention/ppermute | solution.py:361
  51.4 1.9 collective-permute-start.16
  62.5 26.9 %all-to-all-start.2 = ((bf16[16,16,1024]{2,1,0:T(8,128)(2,1)}), bf16[16,16,1024]{2,1,0:T(8,128)(2,1)S(1)}, u32[]{:S(2)}, u32[]{:S(2)}) async-start(bf16[16,16,1024]{2,1,0:T(8,128)(2,1)} %projection.1), calls=%async_computation.2 | async-start | bytes 1048576 | tf_op jit(solution)/shard_map/projection/all_to_all | solution.py:276
  89.6 7.1 %collective-permute-start.19 = (bf16[16,4224]{1,0:T(8,128)(2,1)S(1)}, bf16[16,4224]{1,0:T(8,128)(2,1)S(1)}, u32[]{:S(2)}, u32[]{:S(2)}) collective-permute-start(bf16[16,4224]{1,0:T(8,128)(2,1)S(1)} %get-tuple-element.29.refs_0_), channel_id=1, source_target_pairs={{0,6},{2,0},{4,2},{6,4},{1,7},{3,1},{5,3},{7,5},{8,14},{10,8},{12,... | collective-permute-start | bytes 405512 | tf_op jit(solution)/shard_map/norm/ppermute | solution.py:399
  89.9 7.6 %collective-permute-start.18 = (bf16[16,4224]{1,0:T(8,128)(2,1)S(1)}, bf16[16,4224]{1,0:T(8,128)(2,1)S(1)}, u32[]{:S(2)}, u32[]{:S(2)}) collective-permute-start(bf16[16,4224]{1,0:T(8,128)(2,1)S(1)} %get-tuple-element.29.refs_0_), channel_id=1, source_target_pairs={{0,2},{2,4},{4,6},{6,0},{1,3},{3,5},{5,7},{7,1},{8,10},{10,12},{12... | collective-permute-start | bytes 405512 | tf_op jit(solution)/shard_map/norm/ppermute | solution.py:398
  96.7 7.8 %collective-permute-start.21 = (bf16[16,2176]{1,0:T(8,128)(2,1)S(1)}, bf16[16,2176]{1,0:T(8,128)(2,1)S(1)}, u32[]{:S(2)}, u32[]{:S(2)}) collective-permute-start(bf16[16,2176]{1,0:T(8,128)(2,1)S(1)} %slice.9), channel_id=1, source_target_pairs={{0,6},{2,0},{4,2},{6,4},{1,7},{3,1},{5,3},{7,5},{8,14},{10,8},{12,... | collective-permute-start | bytes 208904 | tf_op jit(solution)/shard_map/norm/ppermute | solution.py:403
  97.5 7.0 %collective-permute-start.20 = (bf16[16,2048]{1,0:T(8,128)(2,1)S(1)}, bf16[16,2048]{1,0:T(8,128)(2,1)S(1)}, u32[]{:S(2)}, u32[]{:S(2)}) collective-permute-start(bf16[16,2048]{1,0:T(8,128)(2,1)S(1)} %slice.8), channel_id=1, source_target_pairs={{0,2},{2,4},{4,6},{6,0},{1,3},{3,5},{5,7},{7,1},{8,10},{10,12},{12... | collective-permute-start | bytes 196616 | tf_op jit(solution)/shard_map/norm/ppermute | solution.py:402
  149.3 31.2 %all-to-all-start.4 = ((bf16[32,8,4096]{2,1,0:T(8,128)(2,1)}), bf16[32,8,4096]{2,1,0:T(8,128)(2,1)S(1)}, u32[]{:S(2)}, u32[]{:S(2)}) async-start(bf16[32,8,4096]{2,1,0:T(8,128)(2,1)} %bitcast.19), calls=%async_computation.4 | async-start | bytes 4194304 | tf_op jit(solution)/shard_map/experts/all_to_all | solution.py:276
  (18 other events, 317.2 us)
where the time goes:
time: 200 us; the launch traced here: 199 us
  waiting for transfers between devices  75.7 us (38%)
  blocking collectives  52.3 us (26%)
  starting transfers between devices  44.3 us (22%)
  Pallas kernels  24.2 us (12%)
    all_to_all x4, waiting for transfers between devices, exchange(): return lax.all_to_all(x, axes, split_axis=0, concat_axis=0, tiled=True)  52.5 us
    all_to_all x2, blocking collectives, exchange(): return lax.all_to_all(x, axes, split_axis=0, concat_axis=0, tiled=True)  52.3 us
    all_to_all x4, starting transfers between devices, exchange(): return lax.all_to_all(x, axes, split_axis=0, concat_axis=0, tiled=True)  25.3 us
    pallas_call x8, Pallas kernels, call(): pl.pallas_call(kernel, out_shape=out_shape, in_specs=specs, out_specs=[wh...  24.2 us
    ppermute x1, waiting for transfers between devices, local(): beside = lax.ppermute(own_half, 'zlo', swap(ZLO))  8.11 us
    ppermute x1, waiting for transfers between devices, local(): far_own = lax.ppermute(left_own, 'cx', ring(CX, 1))  5.63 us
    ppermute x1, waiting for transfers between devices, local(): right = lax.ppermute(ext, 'zhi', ring(ZHI, -1))  4.07 us
  transfers between devices with their start and end apart: 26, of which 12 were waited for; matrix products, arithmetic and copies ran while one was open for 0% of the time, Pallas kernels for 4%

commit v1 on v0

--- a/solution.py
+++ b/solution.py
@@ -18,6 +18,7 @@
 SCORE_FLOOR = -1e30
 LANES = 128
 SUB = 16
+DOWN_PARTS = 4
 MIB = 1024 * 1024
 
 CY, CX, ZHI, ZLO = 4, 4, 4, 2
@@ -101,8 +102,10 @@
     copies = [
         pltpu.make_async_copy(source, held_ref.at[i], sems.at[i]) for i, source in enumerate(sources)
     ]
-    for copy in copies:
-        copy.start()
+    for step in range(CX):
+        for part in range(2):
+            for near in range(ZLO):
+                copies[CX * ZLO * part + ZLO * step + near].start()
     half, width = held_ref.shape[1:]
     rows = att_ref.shape[0] * att_ref.shape[2]
     for step, away in enumerate((0, CX - 1, 1, 2)):
@@ -208,10 +211,25 @@
 
 def expert_kernel(dp_ref, rows_ref, *refs):
     weights, out_ref, held, sems = refs[:6], refs[6], refs[7:13], refs[13]
-    copies = [pltpu.make_async_copy(weights[i], held[i], sems.at[i]) for i in range(6)]
-    for i in (0, 1, 3, 4, 2, 5):
-        copies[i].start()
     model_width = out_ref.shape[1]
+    step = model_width // DOWN_PARTS
+    copies = {i: pltpu.make_async_copy(weights[i], held[i], sems.at[i]) for i in (0, 1, 3, 4)}
+    downs = []
+    for j in range(DOWN_PARTS):
+        columns = pl.ds(j * step, step)
+        downs.append(
+            [
+                pltpu.make_async_copy(
+                    weights[i].at[:, columns], held[i].at[:, columns], sems.at[6 + 2 * j + i // 3]
+                )
+                for i in (2, 5)
+            ]
+        )
+    for copy in copies.values():
+        copy.start()
+    for pair in downs:
+        for copy in pair:
+            copy.start()
     masks = rows_ref[:, model_width:].astype(F32).astype(I32)
     blocks = MASK_BLOCKS // 2
     acts = []
@@ -230,11 +248,10 @@
             [(jnp.right_shift(masks, first + b) & 1).astype(F32) for b in range(blocks)], axis=1
         )
         acts.append((jax.nn.silu(both[:, :units]) * both[:, units:] * keep).astype(BF16))
-    copies[2].wait()
-    copies[5].wait()
     activated = jnp.concatenate(acts, axis=1)
-    step = 512
-    for j in range(model_width // step):
+    for j in range(DOWN_PARTS):
+        for copy in downs[j]:
+            copy.wait()
         columns = slice(j * step, (j + 1) * step)
         down = jnp.concatenate([held[2][:, columns], held[5][:, columns]], axis=0)
         out_ref[:, columns] = jnp.dot(activated, down, preferred_element_type=F32).astype(BF16)
@@ -438,7 +455,7 @@
             vmem=32,
             scalars=(scalar(dp),),
             any_args=[stay(w) if i % 3 == 2 else w for i, w in enumerate(every)],
-            scratch=[pltpu.VMEM(a.shape, a.dtype) for a in every] + [pltpu.SemaphoreType.DMA((6,))],
+            scratch=[pltpu.VMEM(a.shape, a.dtype) for a in every] + [pltpu.SemaphoreType.DMA((6 + 2 * DOWN_PARTS,))],
             flops=6 * slots * model_width * 768,
             moved=22 << 20,
         )

time: 200 us -> 200 us (level)
  no operation moved by 1% of the time
where the time goes in v1:
time: 200 us
  waiting for transfers between devices  75.7 us (38%)
  blocking collectives  52.3 us (26%)
  starting transfers between devices  44.3 us (22%)
  Pallas kernels  24.6 us (12%)
    all_to_all x4, waiting for transfers between devices, exchange(): return lax.all_to_all(x, axes, split_axis=0, concat_axis=0, tiled=True)  52.5 us
    all_to_all x2, blocking collectives, exchange(): return lax.all_to_all(x, axes, split_axis=0, concat_axis=0, tiled=True)  52.3 us
    all_to_all x4, starting transfers between devices, exchange(): return lax.all_to_all(x, axes, split_axis=0, concat_axis=0, tiled=True)  25.3 us
    pallas_call x8, Pallas kernels, call(): pl.pallas_call(kernel, out_shape=out_shape, in_specs=specs, out_specs=[wh...  24.6 us
    ppermute x1, waiting for transfers between devices, local(): beside = lax.ppermute(own_half, 'zlo', swap(ZLO))  8.11 us
    ppermute x1, waiting for transfers between devices, local(): far_own = lax.ppermute(left_own, 'cx', ring(CX, 1))  5.63 us
    ppermute x1, waiting for transfers between devices, local(): right = lax.ppermute(ext, 'zhi', ring(ZHI, -1))  4.07 us
  transfers between devices with their start and end apart: 26, of which 12 were waited for; matrix products, arithmetic and copies ran while one was open for 0% of the time, Pallas kernels for 4%

profile of v1, /device:TPU:32, one launch (start us, length us, event | category | flops | bytes accessed | tf_op | source)
XLA Modules:
  0.0 199.6 jit_solution(6336723328361220880)
XLA Ops:
  0.6 1.9 keys_values.1
  2.5 7.0 %all-to-all-start = ((bf16[16,128,256]{2,1,0:T(8,128)(2,1)}), bf16[16,128,256]{2,1,0:T(8,128)(2,1)S(1)}, u32[]{:S(2)}, u32[]{:S(2)}) async-start(bf16[16,128,256]{2,1,0:T(8,128)(2,1)} %keys_values.1), calls=%async_computation | async-start | bytes 2097152 | tf_op jit(solution)/shard_map/keys_values/all_to_all | solution.py:293
  9.9 8.1 %collective-permute-done.refs_1_ = bf16[512,256]{1,0:T(8,128)(2,1)S(1)} collective-permute-done((bf16[512,256]{1,0:T(8,128)(2,1)S(1)}, bf16[512,256]{1,0:T(8,128)(2,1)S(1)}, u32[]{:S(2)}, u32[]{:S(2)}) %collective-permute-start) | collective-permute-done | bytes 262176 | tf_op jit(solution)/shard_map/out_weight/ppermute | solution.py:342
  18.1 1.6 collective-permute-start.5
  19.7 1.6 collective-permute-start.7
  21.3 7.4 %all-to-all-done.kv_ref = bf16[16,128,256]{2,1,0:T(8,128)(2,1)S(1)} async-done(((bf16[16,128,256]{2,1,0:T(8,128)(2,1)}), bf16[16,128,256]{2,1,0:T(8,128)(2,1)S(1)}, u32[]{:S(2)}, u32[]{:S(2)}) %all-to-all-start) | async-done | bytes 1048608 | tf_op jit(solution)/shard_map/keys_values/all_to_all | solution.py:293
  28.8 3.2 %collective-permute-start.8 = (bf16[512,256]{1,0:T(8,128)(2,1)S(1)}, bf16[512,256]{1,0:T(8,128)(2,1)}, u32[]{:S(2)}, u32[]{:S(2)}) collective-permute-start(bf16[512,256]{1,0:T(8,128)(2,1)S(1)} %collective-permute-done.refs_1_), channel_id=1, source_target_pairs={{0,24},{8,0},{16,8},{24,16},{1,25},{9,1},{17,9},{25,17},{2,26},{10... | collective-permute-start | bytes 786440 | tf_op jit(solution)/shard_map/out_weight/ppermute | solution.py:348
  32.1 5.7 %attention.1 = bf16[8,64,1024]{2,1,0:T(8,128)(2,1)} custom-call(s32[1]{0:T(128)} %bitcast.3.first_ref, bf16[16,128,256]{2,1,0:T(8,128)(2,1)S(1)} %all-to-all-done.kv_ref, s32[128,1]{1,0:T(8,128)S(1)} %copy.14.start_ref, bf16[128,1024]{1,0:T(8,128)(2,1)} %bitcast.39), custom_call_target="tpu_custom_call" | custom-call | flops 1073741824 | bytes 4194304 | tf_op jit(solution)/shard_map/attention/pallas_call | solution.py:35
  37.9 4.0 %all-to-all-start.1 = ((bf16[8,64,1024]{2,1,0:T(8,128)(2,1)}), bf16[8,64,1024]{2,1,0:T(8,128)(2,1)S(1)}, u32[]{:S(2)}, u32[]{:S(2)}) async-start(bf16[8,64,1024]{2,1,0:T(8,128)(2,1)} %attention.1), calls=%async_computation.1 | async-start | bytes 2097152 | tf_op jit(solution)/shard_map/attention/all_to_all | solution.py:293
  42.2 3.0 %collective-permute-start.11 = (bf16[512,256]{1,0:T(8,128)(2,1)}, bf16[512,256]{1,0:T(8,128)(2,1)S(1)}, u32[]{:S(2)}, u32[]{:S(2)}) collective-permute-start(bf16[512,256]{1,0:T(8,128)(2,1)} %collective-permute-done.8.refs_5_), channel_id=1, source_target_pairs={{0,24},{8,0},{16,8},{24,16},{1,25},{9,1},{17,9},{25,17},{2,26},{10... | collective-permute-start | bytes 786440 | tf_op jit(solution)/shard_map/attention/ppermute | solution.py:375
  45.8 5.6 %collective-permute-done.10.refs_6_ = bf16[512,256]{1,0:T(8,128)(2,1)S(1)} collective-permute-done((bf16[512,256]{1,0:T(8,128)(2,1)S(1)}, bf16[512,256]{1,0:T(8,128)(2,1)S(1)}, u32[]{:S(2)}, u32[]{:S(2)}) %collective-permute-start.10) | collective-permute-done | bytes 262176 | tf_op jit(solution)/shard_map/attention/ppermute | solution.py:374
  53.7 3.3 %all-to-all-done.1 = bf16[8,64,1024]{2,1,0:T(8,128)(2,1)S(1)} async-done(((bf16[8,64,1024]{2,1,0:T(8,128)(2,1)}), bf16[8,64,1024]{2,1,0:T(8,128)(2,1)S(1)}, u32[]{:S(2)}, u32[]{:S(2)}) %all-to-all-start.1) | async-done | bytes 1048608 | tf_op jit(solution)/shard_map/attention/all_to_all | solution.py:293
  57.0 5.2 %projection.1 = bf16[16,16,1024]{2,1,0:T(8,128)(2,1)} custom-call(s32[1]{0:T(128)} %bitcast.dp_ref, s32[1]{0:T(128)} %bitcast.1.x_ref, s32[1]{0:T(128)} %bitcast.2.zlo_ref, bf16[4,2,64,1024]{3,2,1,0:T(8,128)(2,1)S(1)} %bitcast.28, bf16[512,256]{1,0:T(8,128)(2,1)} %copy-done.5, bf16[512,256]{1,0:T(8,128)(2,1)} %copy-done.6, bf16[512,256]{1,0:T(8,128)(2,1)} %copy-done.8, ...), custom_call_target="tpu_custom_call" | custom-call | flops 1073741824 | bytes 6291456 | tf_op jit(solution)/shard_map/projection/pallas_call | solution.py:35
  62.2 9.2 %all-to-all-start.2 = ((bf16[16,16,1024]{2,1,0:T(8,128)(2,1)}), bf16[16,16,1024]{2,1,0:T(8,128)(2,1)S(1)}, u32[]{:S(2)}, u32[]{:S(2)}) async-start(bf16[16,16,1024]{2,1,0:T(8,128)(2,1)} %projection.1), calls=%async_computation.2 | async-start | bytes 1048576 | tf_op jit(solution)/shard_map/projection/all_to_all | solution.py:293
  71.7 17.4 %all-to-all-done.2.parts_ref = bf16[16,16,1024]{2,1,0:T(8,128)(2,1)S(1)} async-done(((bf16[16,16,1024]{2,1,0:T(8,128)(2,1)}), bf16[16,16,1024]{2,1,0:T(8,128)(2,1)S(1)}, u32[]{:S(2)}, u32[]{:S(2)}) %all-to-all-start.2) | async-done | bytes 524320 | tf_op jit(solution)/shard_map/projection/all_to_all | solution.py:293
  89.6 2.7 %collective-permute-start.18 = (bf16[16,4224]{1,0:T(8,128)(2,1)S(1)}, bf16[16,4224]{1,0:T(8,128)(2,1)S(1)}, u32[]{:S(2)}, u32[]{:S(2)}) collective-permute-start(bf16[16,4224]{1,0:T(8,128)(2,1)S(1)} %get-tuple-element.29.refs_0_), channel_id=1, source_target_pairs={{0,2},{2,4},{4,6},{6,0},{1,3},{3,5},{5,7},{7,1},{8,10},{10,12},{12... | collective-permute-start | bytes 405512 | tf_op jit(solution)/shard_map/norm/ppermute | solution.py:415
  92.4 4.1 %collective-permute-done.19.refs_2_ = bf16[16,4224]{1,0:T(8,128)(2,1)S(1)} collective-permute-done((bf16[16,4224]{1,0:T(8,128)(2,1)S(1)}, bf16[16,4224]{1,0:T(8,128)(2,1)S(1)}, u32[]{:S(2)}, u32[]{:S(2)}) %collective-permute-start.19) | collective-permute-done | bytes 135200 | tf_op jit(solution)/shard_map/norm/ppermute | solution.py:416
  97.2 3.6 %collective-permute-start.20 = (bf16[16,2048]{1,0:T(8,128)(2,1)S(1)}, bf16[16,2048]{1,0:T(8,128)(2,1)S(1)}, u32[]{:S(2)}, u32[]{:S(2)}) collective-permute-start(bf16[16,2048]{1,0:T(8,128)(2,1)S(1)} %slice.8), channel_id=1, source_target_pairs={{0,2},{2,4},{4,6},{6,0},{1,3},{3,5},{5,7},{7,1},{8,10},{10,12},{12... | collective-permute-start | bytes 196616 | tf_op jit(solution)/shard_map/norm/ppermute | solution.py:419
  100.8 3.4 %collective-permute-done.20.refs_3_ = bf16[16,2048]{1,0:T(8,128)(2,1)S(1)} collective-permute-done((bf16[16,2048]{1,0:T(8,128)(2,1)S(1)}, bf16[16,2048]{1,0:T(8,128)(2,1)S(1)}, u32[]{:S(2)}, u32[]{:S(2)}) %collective-permute-start.20) | collective-permute-done | bytes 65568 | tf_op jit(solution)/shard_map/norm/ppermute | solution.py:419
  105.3 34.9 %all_to_all.30 = bf16[32,8,4224]{2,1,0:T(8,128)(2,1)S(1)} all-to-all(bf16[32,8,4224]{2,1,0:T(8,128)(2,1)S(1)} %bitcast.26), channel_id=1, replica_groups=mesh['dp'=2,'cy'=4,'cx'=4,'zhi'=4,'zlo'=2] {'cy','cx','zlo'}, dimensions={0} | all-to-all | bytes 4325376 | tf_op jit(solution)/shard_map/dispatch/all_to_all | solution.py:293
  140.2 9.4 %experts.1 = bf16[256,4096]{1,0:T(8,128)(2,1)} custom-call(s32[1]{0:T(128)} %bitcast.dp_ref, bf16[256,4224]{1,0:T(8,128)(2,1)S(1)} %bitcast.25, bf16[4096,384]{1,0:T(8,128)(2,1)S(1)} %bitcast.30, bf16[4096,384]{1,0:T(8,128)(2,1)S(1)} %bitcast.32, bf16[384,4096]{1,0:T(8,128)(2,1)} %bitcast.35, bf16[4096,384]{1,0:T(8,128)(2,1)} %collective-permute-done.2.refs_3_, ...), custom_call_target="tpu_custom_call" | custom-call | flops 4831838208 | bytes 23068672 | tf_op jit(solution)/shard_map/experts/pallas_call | solution.py:35
  149.6 5.0 %all-to-all-start.4 = ((bf16[32,8,4096]{2,1,0:T(8,128)(2,1)}), bf16[32,8,4096]{2,1,0:T(8,128)(2,1)S(1)}, u32[]{:S(2)}, u32[]{:S(2)}) async-start(bf16[32,8,4096]{2,1,0:T(8,128)(2,1)} %bitcast.19), calls=%async_computation.4 | async-start | bytes 4194304 | tf_op jit(solution)/shard_map/experts/all_to_all | solution.py:293
  156.4 24.4 %all-to-all-done.4 = bf16[32,8,4096]{2,1,0:T(8,128)(2,1)S(1)} async-done(((bf16[32,8,4096]{2,1,0:T(8,128)(2,1)}), bf16[32,8,4096]{2,1,0:T(8,128)(2,1)S(1)}, u32[]{:S(2)}, u32[]{:S(2)}) %all-to-all-start.4) | async-done | bytes 2097184 | tf_op jit(solution)/shard_map/experts/all_to_all | solution.py:293
  181.4 17.4 %all_to_all.31 = bf16[4,16,4096]{2,1,0:T(8,128)(2,1)S(1)} all-to-all(bf16[4,16,4096]{2,1,0:T(8,128)(2,1)S(1)} %combine.1), channel_id=1, replica_groups=mesh['dp'=2,'cy'=4,'cx'=4,'zhi'=4,'zlo'=2] {'zhi'}, dimensions={0} | all-to-all | bytes 1048576 | tf_op jit(solution)/shard_map/combine/all_to_all | solution.py:293
  (82 shorter events, 10.1 us)
Async XLA Ops:
  0.0 28.7 %collective-permute-start.2 = (bf16[4096,384]{1,0:T(8,128)(2,1)}, bf16[4096,384]{1,0:T(8,128)(2,1)}, u32[]{:S(2)}, u32[]{:S(2)}) collective-permute-start(bf16[4096,384]{1,0:T(8,128)(2,1)} %bitcast.29), channel_id=1, source_target_pairs={{0,128},{128,0},{1,129},{129,1},{2,130},{130,2},{3,131},{131,3},{4... | collective-permute-start | bytes 9437192 | tf_op jit(solution)/shard_map/expert_weights/ppermute | solution.py:337
  0.0 28.7 %collective-permute-start.3 = (bf16[4096,384]{1,0:T(8,128)(2,1)}, bf16[4096,384]{1,0:T(8,128)(2,1)}, u32[]{:S(2)}, u32[]{:S(2)}) collective-permute-start(bf16[4096,384]{1,0:T(8,128)(2,1)} %bitcast.31), channel_id=1, source_target_pairs={{0,128},{128,0},{1,129},{129,1},{2,130},{130,2},{3,131},{131,3},{4... | collective-permute-start | bytes 9437192 | tf_op jit(solution)/shard_map/expert_weights/ppermute | solution.py:337
  0.5 28.2 %collective-permute-start.4 = (bf16[384,4096]{1,0:T(8,128)(2,1)}, bf16[384,4096]{1,0:T(8,128)(2,1)}, u32[]{:S(2)}, u32[]{:S(2)}) collective-permute-start(bf16[384,4096]{1,0:T(8,128)(2,1)} %bitcast.34), channel_id=1, source_target_pairs={{0,128},{128,0},{1,129},{129,1},{2,130},{130,2},{3,131},{131,3},{4... | collective-permute-start | bytes 9437192 | tf_op jit(solution)/shard_map/expert_weights/ppermute | solution.py:337
  2.5 26.2 %all-to-all-start = ((bf16[16,128,256]{2,1,0:T(8,128)(2,1)}), bf16[16,128,256]{2,1,0:T(8,128)(2,1)S(1)}, u32[]{:S(2)}, u32[]{:S(2)}) async-start(bf16[16,128,256]{2,1,0:T(8,128)(2,1)} %keys_values.1), calls=%async_computation | async-start | bytes 2097152 | tf_op jit(solution)/shard_map/keys_values/all_to_all | solution.py:293
  9.6 8.4 %collective-permute-start = (bf16[512,256]{1,0:T(8,128)(2,1)S(1)}, bf16[512,256]{1,0:T(8,128)(2,1)S(1)}, u32[]{:S(2)}, u32[]{:S(2)}) collective-permute-start(bf16[512,256]{1,0:T(8,128)(2,1)S(1)} %constant_dynamic-slice_fusion.refs_0_), channel_id=1, source_target_pairs={{0,1},{1,0},{2,3},{3,2},{4,5},{5,4},{6,7},{7,6},{8,9},{9,8},{10,11... | collective-permute-start | bytes 786440 | tf_op jit(solution)/shard_map/out_weight/ppermute | solution.py:342
  9.8 9.9 %collective-permute-start.1 = (bf16[512,256]{1,0:T(8,128)(2,1)S(1)}, bf16[512,256]{1,0:T(8,128)(2,1)S(1)}, u32[]{:S(2)}, u32[]{:S(2)}) collective-permute-start(bf16[512,256]{1,0:T(8,128)(2,1)S(1)} %constant_dynamic-slice_fusion.refs_0_), channel_id=1, source_target_pairs={{0,128},{128,0},{1,129},{129,1},{2,130},{130,2},{3,131},{131,3},{4... | collective-permute-start | bytes 786440 | tf_op jit(solution)/shard_map/out_weight/ppermute | solution.py:343
  18.1 19.7 %collective-permute-start.5 = (bf16[512,256]{1,0:T(8,128)(2,1)S(1)}, bf16[512,256]{1,0:T(8,128)(2,1)S(1)}, u32[]{:S(2)}, u32[]{:S(2)}) collective-permute-start(bf16[512,256]{1,0:T(8,128)(2,1)S(1)} %constant_dynamic-slice_fusion.refs_0_), channel_id=1, source_target_pairs={{0,8},{8,16},{16,24},{24,0},{1,9},{9,17},{17,25},{25,1},{2,10},{10... | collective-permute-start | bytes 786440 | tf_op jit(solution)/shard_map/out_weight/ppermute | solution.py:347
  19.7 18.1 %collective-permute-start.7 = (bf16[512,256]{1,0:T(8,128)(2,1)S(1)}, bf16[512,256]{1,0:T(8,128)(2,1)}, u32[]{:S(2)}, u32[]{:S(2)}) collective-permute-start(bf16[512,256]{1,0:T(8,128)(2,1)S(1)} %constant_dynamic-slice_fusion.refs_0_), channel_id=1, source_target_pairs={{0,24},{8,0},{16,8},{24,16},{1,25},{9,1},{17,9},{25,17},{2,26},{10... | collective-permute-start | bytes 786440 | tf_op jit(solution)/shard_map/out_weight/ppermute | solution.py:350
  28.7 9.1 %collective-permute-start.6 = (bf16[512,256]{1,0:T(8,128)(2,1)S(1)}, bf16[512,256]{1,0:T(8,128)(2,1)}, u32[]{:S(2)}, u32[]{:S(2)}) collective-permute-start(bf16[512,256]{1,0:T(8,128)(2,1)S(1)} %collective-permute-done.refs_1_), channel_id=1, source_target_pairs={{0,8},{8,16},{16,24},{24,0},{1,9},{9,17},{17,25},{25,1},{2,10},{10... | collective-permute-start | bytes 786440 | tf_op jit(solution)/shard_map/out_weight/ppermute | solution.py:349
  28.8 9.0 %collective-permute-start.8 = (bf16[512,256]{1,0:T(8,128)(2,1)S(1)}, bf16[512,256]{1,0:T(8,128)(2,1)}, u32[]{:S(2)}, u32[]{:S(2)}) collective-permute-start(bf16[512,256]{1,0:T(8,128)(2,1)S(1)} %collective-permute-done.refs_1_), channel_id=1, source_target_pairs={{0,24},{8,0},{16,8},{24,16},{1,25},{9,1},{17,9},{25,17},{2,26},{10... | collective-permute-start | bytes 786440 | tf_op jit(solution)/shard_map/out_weight/ppermute | solution.py:348
  32.0 5.8 %collective-permute-start.9 = (bf16[512,256]{1,0:T(8,128)(2,1)S(1)}, bf16[512,256]{1,0:T(8,128)(2,1)S(1)}, u32[]{:S(2)}, u32[]{:S(2)}) collective-permute-start(bf16[512,256]{1,0:T(8,128)(2,1)S(1)} %collective-permute-done.refs_1_), channel_id=1, source_target_pairs={{0,128},{128,0},{1,129},{129,1},{2,130},{130,2},{3,131},{131,3},{4... | collective-permute-start | bytes 786440 | tf_op jit(solution)/shard_map/out_weight/ppermute | solution.py:351
  37.9 19.1 %all-to-all-start.1 = ((bf16[8,64,1024]{2,1,0:T(8,128)(2,1)}), bf16[8,64,1024]{2,1,0:T(8,128)(2,1)S(1)}, u32[]{:S(2)}, u32[]{:S(2)}) async-start(bf16[8,64,1024]{2,1,0:T(8,128)(2,1)} %attention.1), calls=%async_computation.1 | async-start | bytes 2097152 | tf_op jit(solution)/shard_map/attention/all_to_all | solution.py:293
  41.9 9.5 %collective-permute-start.10 = (bf16[512,256]{1,0:T(8,128)(2,1)S(1)}, bf16[512,256]{1,0:T(8,128)(2,1)S(1)}, u32[]{:S(2)}, u32[]{:S(2)}) collective-permute-start(bf16[512,256]{1,0:T(8,128)(2,1)S(1)} %collective-permute-done.5.refs_2_), channel_id=1, source_target_pairs={{0,8},{8,16},{16,24},{24,0},{1,9},{9,17},{17,25},{25,1},{2,10},{10... | collective-permute-start | bytes 786440 | tf_op jit(solution)/shard_map/attention/ppermute | solution.py:374
  42.2 9.3 %collective-permute-start.11 = (bf16[512,256]{1,0:T(8,128)(2,1)}, bf16[512,256]{1,0:T(8,128)(2,1)S(1)}, u32[]{:S(2)}, u32[]{:S(2)}) collective-permute-start(bf16[512,256]{1,0:T(8,128)(2,1)} %collective-permute-done.8.refs_5_), channel_id=1, source_target_pairs={{0,24},{8,0},{16,8},{24,16},{1,25},{9,1},{17,9},{25,17},{2,26},{10... | collective-permute-start | bytes 786440 | tf_op jit(solution)/shard_map/attention/ppermute | solution.py:375
  45.2 6.8 %collective-permute-start.12 = (bf16[512,256]{1,0:T(8,128)(2,1)S(1)}, bf16[512,256]{1,0:T(8,128)(2,1)S(1)}, u32[]{:S(2)}, u32[]{:S(2)}) collective-permute-start(bf16[512,256]{1,0:T(8,128)(2,1)S(1)} %collective-permute-done.5.refs_2_), channel_id=1, source_target_pairs={{0,128},{128,0},{1,129},{129,1},{2,130},{130,2},{3,131},{131,3},{4... | collective-permute-start | bytes 786440 | tf_op jit(solution)/shard_map/attention/ppermute | solution.py:378
  45.2 8.0 %collective-permute-start.15 = (bf16[512,256]{1,0:T(8,128)(2,1)}, bf16[512,256]{1,0:T(8,128)(2,1)S(1)}, u32[]{:S(2)}, u32[]{:S(2)}) collective-permute-start(bf16[512,256]{1,0:T(8,128)(2,1)} %collective-permute-done.8.refs_5_), channel_id=1, source_target_pairs={{0,128},{128,0},{1,129},{129,1},{2,130},{130,2},{3,131},{131,3},{4... | collective-permute-start | bytes 786440 | tf_op jit(solution)/shard_map/attention/ppermute | solution.py:378
  45.7 6.4 %collective-permute-start.13 = (bf16[512,256]{1,0:T(8,128)(2,1)}, bf16[512,256]{1,0:T(8,128)(2,1)S(1)}, u32[]{:S(2)}, u32[]{:S(2)}) collective-permute-start(bf16[512,256]{1,0:T(8,128)(2,1)} %collective-permute-done.6.refs_3_), channel_id=1, source_target_pairs={{0,128},{128,0},{1,129},{129,1},{2,130},{130,2},{3,131},{131,3},{4... | collective-permute-start | bytes 786440 | tf_op jit(solution)/shard_map/attention/ppermute | solution.py:378
  51.4 1.9 collective-permute-start.16
  62.2 26.9 %all-to-all-start.2 = ((bf16[16,16,1024]{2,1,0:T(8,128)(2,1)}), bf16[16,16,1024]{2,1,0:T(8,128)(2,1)S(1)}, u32[]{:S(2)}, u32[]{:S(2)}) async-start(bf16[16,16,1024]{2,1,0:T(8,128)(2,1)} %projection.1), calls=%async_computation.2 | async-start | bytes 1048576 | tf_op jit(solution)/shard_map/projection/all_to_all | solution.py:293
  89.3 7.1 %collective-permute-start.19 = (bf16[16,4224]{1,0:T(8,128)(2,1)S(1)}, bf16[16,4224]{1,0:T(8,128)(2,1)S(1)}, u32[]{:S(2)}, u32[]{:S(2)}) collective-permute-start(bf16[16,4224]{1,0:T(8,128)(2,1)S(1)} %get-tuple-element.29.refs_0_), channel_id=1, source_target_pairs={{0,6},{2,0},{4,2},{6,4},{1,7},{3,1},{5,3},{7,5},{8,14},{10,8},{12,... | collective-permute-start | bytes 405512 | tf_op jit(solution)/shard_map/norm/ppermute | solution.py:416
  89.6 7.6 %collective-permute-start.18 = (bf16[16,4224]{1,0:T(8,128)(2,1)S(1)}, bf16[16,4224]{1,0:T(8,128)(2,1)S(1)}, u32[]{:S(2)}, u32[]{:S(2)}) collective-permute-start(bf16[16,4224]{1,0:T(8,128)(2,1)S(1)} %get-tuple-element.29.refs_0_), channel_id=1, source_target_pairs={{0,2},{2,4},{4,6},{6,0},{1,3},{3,5},{5,7},{7,1},{8,10},{10,12},{12... | collective-permute-start | bytes 405512 | tf_op jit(solution)/shard_map/norm/ppermute | solution.py:415
  96.4 7.8 %collective-permute-start.21 = (bf16[16,2176]{1,0:T(8,128)(2,1)S(1)}, bf16[16,2176]{1,0:T(8,128)(2,1)S(1)}, u32[]{:S(2)}, u32[]{:S(2)}) collective-permute-start(bf16[16,2176]{1,0:T(8,128)(2,1)S(1)} %slice.9), channel_id=1, source_target_pairs={{0,6},{2,0},{4,2},{6,4},{1,7},{3,1},{5,3},{7,5},{8,14},{10,8},{12,... | collective-permute-start | bytes 208904 | tf_op jit(solution)/shard_map/norm/ppermute | solution.py:420
  97.2 7.0 %collective-permute-start.20 = (bf16[16,2048]{1,0:T(8,128)(2,1)S(1)}, bf16[16,2048]{1,0:T(8,128)(2,1)S(1)}, u32[]{:S(2)}, u32[]{:S(2)}) collective-permute-start(bf16[16,2048]{1,0:T(8,128)(2,1)S(1)} %slice.8), channel_id=1, source_target_pairs={{0,2},{2,4},{4,6},{6,0},{1,3},{3,5},{5,7},{7,1},{8,10},{10,12},{12... | collective-permute-start | bytes 196616 | tf_op jit(solution)/shard_map/norm/ppermute | solution.py:419
  149.6 31.2 %all-to-all-start.4 = ((bf16[32,8,4096]{2,1,0:T(8,128)(2,1)}), bf16[32,8,4096]{2,1,0:T(8,128)(2,1)S(1)}, u32[]{:S(2)}, u32[]{:S(2)}) async-start(bf16[32,8,4096]{2,1,0:T(8,128)(2,1)} %bitcast.19), calls=%async_computation.4 | async-start | bytes 4194304 | tf_op jit(solution)/shard_map/experts/all_to_all | solution.py:293
  (18 other events, 316.2 us)

commit v2 on v0

--- a/solution.py
+++ b/solution.py
@@ -92,7 +92,7 @@
                 block = attended[which * tokens + z * SUB : which * tokens + (z + 1) * SUB]
                 rows = slice((z // ZLO) * SUB, (z // ZLO + 1) * SUB)
                 for y in range(CY):
-                    out_ref[y * ZLO + z % ZLO, rows, columns[which]] = block
+                    out_ref[z % ZLO * CY + y, rows, columns[which]] = block
 
 
 def project_kernel(dp_ref, x_ref, zlo_ref, att_ref, *refs):
@@ -104,7 +104,7 @@
     for copy in copies:
         copy.start()
     half, width = held_ref.shape[1:]
-    rows = att_ref.shape[0] * att_ref.shape[2]
+    rows = att_ref.shape[1] * att_ref.shape[2]
     for step, away in enumerate((0, CX - 1, 1, 2)):
         total = jnp.zeros((rows, width), F32)
         for part in range(2):
@@ -116,12 +116,15 @@
                 piece = CX * ZLO * part + ZLO * step + near
                 copies[piece].wait()
                 total += jnp.dot(
-                    att_ref[:, source, :, columns].reshape(rows, half),
+                    att_ref[source, :, :, columns].reshape(rows, half),
                     held_ref[piece],
                     preferred_element_type=F32,
                 )
         place = pl.multiple_of(((x_ref[0] + away) & (CX - 1)) * width, width)
-        out_ref[:, :, pl.ds(place, width)] = total.astype(BF16).reshape(rows // SUB, SUB, width)
+        total = total.astype(BF16).reshape(rows // SUB, SUB, width)
+        for y in range(CY):
+            for z in range(ZHI):
+                out_ref[z * CY + y, :, pl.ds(place, width)] = total[y * ZHI + z]
 
 
 def norm_kernel(parts_ref, residual_ref, gain_ref, meta_ref, ext_ref, hidden_ref):
@@ -132,7 +135,7 @@
     square_sum = jnp.zeros((SUB, 1), F32)
     for y in range(CY):
         columns = slice(y * width, (y + 1) * width)
-        projected = sum(parts_ref[y * zs + z].astype(F32) for z in range(zs))
+        projected = sum(parts_ref[z * CY + y].astype(F32) for z in range(zs))
         hidden = (residual_ref[:, columns].astype(F32) + projected).astype(BF16)
         hidden_ref[:, columns] = hidden
         wide = hidden.astype(F32)
@@ -150,7 +153,8 @@
     tokens = meta.shape[0]
     slot = lax.broadcasted_iota(I32, (tokens, slots), 1)
     dest = slot >> (slot_capacity.bit_length() - 1)
-    expert = (dest >> 1) * (ZHI * ZLO) + zhi * ZLO + (dest & 1)
+    ctx = (dest >> 3) * CX + (dest & (CX - 1))
+    expert = ctx * (ZHI * ZLO) + zhi * ZLO + ((dest >> 2) & (ZLO - 1))
     hits = [meta[:, k : k + 1].astype(F32).astype(I32) == expert for k in range(TOP)]
     named = sum(h.astype(F32) for h in hits)
     later = lax.broadcasted_iota(I32, (tokens, tokens), 0) > lax.broadcasted_iota(
@@ -359,8 +363,8 @@
         near = [own_half, beside]
         later = [left_own, left_beside, right_own, right_beside, far_own, far_beside]
         others = [own_other, beside_other] + [lax.ppermute(w, "dp", swap(2)) for w in later]
-        gathered = exchange(attended, ("cy", "zlo"))
-        gathered = gathered.reshape(CY, ZLO, tokens // ZLO, queries.shape[2])
+        gathered = exchange(attended, ("zlo", "cy"))
+        gathered = gathered.reshape(ZLO, CY, tokens // ZLO, queries.shape[2])
 
     with jax.named_scope("projection"):
         half, width = out_weight.shape[0] // 2, out_weight.shape[1]
@@ -380,7 +384,7 @@
             flops=2 * group_rows * 16 * half * width,
             moved=6 << 20,
         )
-        parts = exchange(partial, ("cy", "zhi"))
+        parts = exchange(partial, ("zhi", "cy"))
 
     with jax.named_scope("norm"):
         meta = jnp.concatenate([routes[0], block_masks[0]], axis=1).astype(BF16)
@@ -426,7 +430,7 @@
             flops=2 * 64 * EXPERTS * model_width,
             moved=2 << 20,
         )
-        over = ("cy", "cx", "zlo")
+        over = ("cy", "zlo", "cx")
         got = exchange(rows.reshape(dests, capacity, model_width + LANES), over)
 
     with jax.named_scope("experts"):

time: 200 us -> 201 us (level)
  waiting for transfers between devices: 75.7 us -> 78.6 us
  blocking collectives: 52.3 us -> 50.2 us
    ppermute x1, starting transfers between devices: 3.59 us -> 0.01 us  [local(): lax.ppermute(left[:, :cut], 'zhi', ring(ZHI, 1))]
    ppermute x1, waiting for transfers between devices: 3.37 us -> 6.37 us  [local(): lax.ppermute(left[:, :cut], 'zhi', ring(ZHI, 1))]
    ppermute x1, starting transfers between devices: 0.44 us -> 2.71 us  [local(): lax.ppermute(right[:, cut:], 'zhi', ring(ZHI, -1))]
    all_to_all x2, blocking collectives: 52.3 us -> 50.2 us  [exchange(): return lax.all_to_all(x, axes, split_axis=0, concat_axis=0, tiled=True)]
where the time goes in v2:
time: 201 us; the launch traced here: 199 us
  waiting for transfers between devices  78.6 us (39%)
  blocking collectives  50.2 us (25%)
  starting transfers between devices  43.4 us (22%)
  Pallas kernels  24.2 us (12%)
    all_to_all x4, waiting for transfers between devices, exchange(): return lax.all_to_all(x, axes, split_axis=0, concat_axis=0, tiled=True)  51.2 us
    all_to_all x2, blocking collectives, exchange(): return lax.all_to_all(x, axes, split_axis=0, concat_axis=0, tiled=True)  50.2 us
    all_to_all x4, starting transfers between devices, exchange(): return lax.all_to_all(x, axes, split_axis=0, concat_axis=0, tiled=True)  25.8 us
    pallas_call x8, Pallas kernels, call(): pl.pallas_call(kernel, out_shape=out_shape, in_specs=specs, out_specs=[wh...  24.2 us
    ppermute x1, waiting for transfers between devices, local(): beside = lax.ppermute(own_half, 'zlo', swap(ZLO))  8.11 us
    ppermute x1, waiting for transfers between devices, local(): lax.ppermute(left[:, :cut], 'zhi', ring(ZHI, 1))  6.37 us
    ppermute x1, waiting for transfers between devices, local(): far_own = lax.ppermute(left_own, 'cx', ring(CX, 1))  5.63 us
    ppermute x1, waiting for transfers between devices, local(): right = lax.ppermute(ext, 'zhi', ring(ZHI, -1))  4.4 us
  transfers between devices with their start and end apart: 26, of which 12 were waited for; matrix products, arithmetic and copies ran while one was open for 0% of the time, Pallas kernels for 4%

profile of v2, /device:TPU:32, one launch (start us, length us, event | category | flops | bytes accessed | tf_op | source)
XLA Modules:
  0.0 199.2 jit_solution(5295615467787403108)
XLA Ops:
  0.6 1.9 keys_values.1
  2.5 7.0 %all-to-all-start = ((bf16[16,128,256]{2,1,0:T(8,128)(2,1)}), bf16[16,128,256]{2,1,0:T(8,128)(2,1)S(1)}, u32[]{:S(2)}, u32[]{:S(2)}) async-start(bf16[16,128,256]{2,1,0:T(8,128)(2,1)} %keys_values.1), calls=%async_computation | async-start | bytes 2097152 | tf_op jit(solution)/shard_map/keys_values/all_to_all | solution.py:280
  9.9 8.1 %collective-permute-done.refs_1_ = bf16[512,256]{1,0:T(8,128)(2,1)S(1)} collective-permute-done((bf16[512,256]{1,0:T(8,128)(2,1)S(1)}, bf16[512,256]{1,0:T(8,128)(2,1)S(1)}, u32[]{:S(2)}, u32[]{:S(2)}) %collective-permute-start) | collective-permute-done | bytes 262176 | tf_op jit(solution)/shard_map/out_weight/ppermute | solution.py:329
  18.1 1.6 collective-permute-start.5
  19.7 1.6 collective-permute-start.7
  21.3 7.4 %all-to-all-done.kv_ref = bf16[16,128,256]{2,1,0:T(8,128)(2,1)S(1)} async-done(((bf16[16,128,256]{2,1,0:T(8,128)(2,1)}), bf16[16,128,256]{2,1,0:T(8,128)(2,1)S(1)}, u32[]{:S(2)}, u32[]{:S(2)}) %all-to-all-start) | async-done | bytes 1048608 | tf_op jit(solution)/shard_map/keys_values/all_to_all | solution.py:280
  28.8 3.2 %collective-permute-start.8 = (bf16[512,256]{1,0:T(8,128)(2,1)S(1)}, bf16[512,256]{1,0:T(8,128)(2,1)}, u32[]{:S(2)}, u32[]{:S(2)}) collective-permute-start(bf16[512,256]{1,0:T(8,128)(2,1)S(1)} %collective-permute-done.refs_1_), channel_id=1, source_target_pairs={{0,24},{8,0},{16,8},{24,16},{1,25},{9,1},{17,9},{25,17},{2,26},{10... | collective-permute-start | bytes 786440 | tf_op jit(solution)/shard_map/out_weight/ppermute | solution.py:335
  32.1 5.7 %attention.1 = bf16[8,64,1024]{2,1,0:T(8,128)(2,1)} custom-call(s32[1]{0:T(128)} %bitcast.3.first_ref, bf16[16,128,256]{2,1,0:T(8,128)(2,1)S(1)} %all-to-all-done.kv_ref, s32[128,1]{1,0:T(8,128)S(1)} %copy.14.start_ref, bf16[128,1024]{1,0:T(8,128)(2,1)} %bitcast.39), custom_call_target="tpu_custom_call" | custom-call | flops 1073741824 | bytes 4194304 | tf_op jit(solution)/shard_map/attention/pallas_call | solution.py:34
  37.9 4.1 %all-to-all-start.1 = ((bf16[8,64,1024]{2,1,0:T(8,128)(2,1)}), bf16[8,64,1024]{2,1,0:T(8,128)(2,1)S(1)}, u32[]{:S(2)}, u32[]{:S(2)}) async-start(bf16[8,64,1024]{2,1,0:T(8,128)(2,1)} %attention.1), calls=%async_computation.1 | async-start | bytes 2097152 | tf_op jit(solution)/shard_map/attention/all_to_all | solution.py:280
  42.2 3.0 %collective-permute-start.11 = (bf16[512,256]{1,0:T(8,128)(2,1)}, bf16[512,256]{1,0:T(8,128)(2,1)S(1)}, u32[]{:S(2)}, u32[]{:S(2)}) collective-permute-start(bf16[512,256]{1,0:T(8,128)(2,1)} %collective-permute-done.8.refs_5_), channel_id=1, source_target_pairs={{0,24},{8,0},{16,8},{24,16},{1,25},{9,1},{17,9},{25,17},{2,26},{10... | collective-permute-start | bytes 786440 | tf_op jit(solution)/shard_map/attention/ppermute | solution.py:362
  45.8 5.6 %collective-permute-done.10.refs_6_ = bf16[512,256]{1,0:T(8,128)(2,1)S(1)} collective-permute-done((bf16[512,256]{1,0:T(8,128)(2,1)S(1)}, bf16[512,256]{1,0:T(8,128)(2,1)S(1)}, u32[]{:S(2)}, u32[]{:S(2)}) %collective-permute-start.10) | collective-permute-done | bytes 262176 | tf_op jit(solution)/shard_map/attention/ppermute | solution.py:361
  53.7 3.0 %all-to-all-done.1 = bf16[8,64,1024]{2,1,0:T(8,128)(2,1)S(1)} async-done(((bf16[8,64,1024]{2,1,0:T(8,128)(2,1)}), bf16[8,64,1024]{2,1,0:T(8,128)(2,1)S(1)}, u32[]{:S(2)}, u32[]{:S(2)}) %all-to-all-start.1) | async-done | bytes 1048608 | tf_op jit(solution)/shard_map/attention/all_to_all | solution.py:280
  56.7 5.5 %projection.1 = bf16[16,16,1024]{2,1,0:T(8,128)(2,1)} custom-call(s32[1]{0:T(128)} %bitcast.dp_ref, s32[1]{0:T(128)} %bitcast.1.x_ref, s32[1]{0:T(128)} %bitcast.2.zlo_ref, bf16[2,4,64,1024]{3,2,1,0:T(8,128)(2,1)S(1)} %bitcast.28, bf16[512,256]{1,0:T(8,128)(2,1)} %copy-done.5, bf16[512,256]{1,0:T(8,128)(2,1)} %copy-done.6, bf16[512,256]{1,0:T(8,128)(2,1)} %copy-done.8, ...), custom_call_target="tpu_custom_call" | custom-call | flops 1073741824 | bytes 6291456 | tf_op jit(solution)/shard_map/projection/pallas_call | solution.py:34
  62.2 9.4 %all-to-all-start.2 = ((bf16[16,16,1024]{2,1,0:T(8,128)(2,1)}), bf16[16,16,1024]{2,1,0:T(8,128)(2,1)S(1)}, u32[]{:S(2)}, u32[]{:S(2)}) async-start(bf16[16,16,1024]{2,1,0:T(8,128)(2,1)} %projection.1), calls=%async_computation.2 | async-start | bytes 1048576 | tf_op jit(solution)/shard_map/projection/all_to_all | solution.py:280
  72.0 18.1 %all-to-all-done.2.parts_ref = bf16[16,16,1024]{2,1,0:T(8,128)(2,1)S(1)} async-done(((bf16[16,16,1024]{2,1,0:T(8,128)(2,1)}), bf16[16,16,1024]{2,1,0:T(8,128)(2,1)S(1)}, u32[]{:S(2)}, u32[]{:S(2)}) %all-to-all-start.2) | async-done | bytes 524320 | tf_op jit(solution)/shard_map/projection/all_to_all | solution.py:280
  90.3 2.3 %collective-permute-start.19 = (bf16[16,4224]{1,0:T(8,128)(2,1)S(1)}, bf16[16,4224]{1,0:T(8,128)(2,1)S(1)}, u32[]{:S(2)}, u32[]{:S(2)}) collective-permute-start(bf16[16,4224]{1,0:T(8,128)(2,1)S(1)} %get-tuple-element.29.refs_0_), channel_id=1, source_target_pairs={{0,6},{2,0},{4,2},{6,4},{1,7},{3,1},{5,3},{7,5},{8,14},{10,8},{12,... | collective-permute-start | bytes 405512 | tf_op jit(solution)/shard_map/norm/ppermute | solution.py:403
  93.3 4.4 %collective-permute-done.19.refs_2_ = bf16[16,4224]{1,0:T(8,128)(2,1)S(1)} collective-permute-done((bf16[16,4224]{1,0:T(8,128)(2,1)S(1)}, bf16[16,4224]{1,0:T(8,128)(2,1)S(1)}, u32[]{:S(2)}, u32[]{:S(2)}) %collective-permute-start.19) | collective-permute-done | bytes 135200 | tf_op jit(solution)/shard_map/norm/ppermute | solution.py:403
  97.7 2.7 %collective-permute-start.21 = (bf16[16,2176]{1,0:T(8,128)(2,1)S(1)}, bf16[16,2176]{1,0:T(8,128)(2,1)S(1)}, u32[]{:S(2)}, u32[]{:S(2)}) collective-permute-start(bf16[16,2176]{1,0:T(8,128)(2,1)S(1)} %slice.9), channel_id=1, source_target_pairs={{0,6},{2,0},{4,2},{6,4},{1,7},{3,1},{5,3},{7,5},{8,14},{10,8},{12,... | collective-permute-start | bytes 208904 | tf_op jit(solution)/shard_map/norm/ppermute | solution.py:407
  101.6 6.4 %collective-permute-done.20.refs_3_ = bf16[16,2048]{1,0:T(8,128)(2,1)S(1)} collective-permute-done((bf16[16,2048]{1,0:T(8,128)(2,1)S(1)}, bf16[16,2048]{1,0:T(8,128)(2,1)S(1)}, u32[]{:S(2)}, u32[]{:S(2)}) %collective-permute-start.20) | collective-permute-done | bytes 65568 | tf_op jit(solution)/shard_map/norm/ppermute | solution.py:406
  109.0 30.7 %all_to_all.30 = bf16[32,8,4224]{2,1,0:T(8,128)(2,1)S(1)} all-to-all(bf16[32,8,4224]{2,1,0:T(8,128)(2,1)S(1)} %bitcast.26), channel_id=1, replica_groups=mesh['dp'=2,'cy'=4,'cx'=4,'zhi'=4,'zlo'=2] {'cy','zlo','cx'}, dimensions={0} | all-to-all | bytes 4325376 | tf_op jit(solution)/shard_map/dispatch/all_to_all | solution.py:280
  139.8 8.8 %experts.1 = bf16[256,4096]{1,0:T(8,128)(2,1)} custom-call(s32[1]{0:T(128)} %bitcast.dp_ref, bf16[256,4224]{1,0:T(8,128)(2,1)S(1)} %bitcast.25, bf16[4096,384]{1,0:T(8,128)(2,1)S(1)} %bitcast.30, bf16[4096,384]{1,0:T(8,128)(2,1)S(1)} %bitcast.32, bf16[384,4096]{1,0:T(8,128)(2,1)} %bitcast.35, bf16[4096,384]{1,0:T(8,128)(2,1)} %collective-permute-done.2.refs_3_, ...), custom_call_target="tpu_custom_call" | custom-call | flops 4831838208 | bytes 23068672 | tf_op jit(solution)/shard_map/experts/pallas_call | solution.py:34
  148.6 5.2 %all-to-all-start.4 = ((bf16[32,8,4096]{2,1,0:T(8,128)(2,1)}), bf16[32,8,4096]{2,1,0:T(8,128)(2,1)S(1)}, u32[]{:S(2)}, u32[]{:S(2)}) async-start(bf16[32,8,4096]{2,1,0:T(8,128)(2,1)} %bitcast.19), calls=%async_computation.4 | async-start | bytes 4194304 | tf_op jit(solution)/shard_map/experts/all_to_all | solution.py:280
  155.6 22.8 %all-to-all-done.4 = bf16[32,8,4096]{2,1,0:T(8,128)(2,1)S(1)} async-done(((bf16[32,8,4096]{2,1,0:T(8,128)(2,1)}), bf16[32,8,4096]{2,1,0:T(8,128)(2,1)S(1)}, u32[]{:S(2)}, u32[]{:S(2)}) %all-to-all-start.4) | async-done | bytes 2097184 | tf_op jit(solution)/shard_map/experts/all_to_all | solution.py:280
  179.0 19.4 %all_to_all.31 = bf16[4,16,4096]{2,1,0:T(8,128)(2,1)S(1)} all-to-all(bf16[4,16,4096]{2,1,0:T(8,128)(2,1)S(1)} %combine.1), channel_id=1, replica_groups=mesh['dp'=2,'cy'=4,'cx'=4,'zhi'=4,'zlo'=2] {'zhi'}, dimensions={0} | all-to-all | bytes 1048576 | tf_op jit(solution)/shard_map/combine/all_to_all | solution.py:280
  (82 shorter events, 11.0 us)
Async XLA Ops:
  0.0 28.7 %collective-permute-start.2 = (bf16[4096,384]{1,0:T(8,128)(2,1)}, bf16[4096,384]{1,0:T(8,128)(2,1)}, u32[]{:S(2)}, u32[]{:S(2)}) collective-permute-start(bf16[4096,384]{1,0:T(8,128)(2,1)} %bitcast.29), channel_id=1, source_target_pairs={{0,128},{128,0},{1,129},{129,1},{2,130},{130,2},{3,131},{131,3},{4... | collective-permute-start | bytes 9437192 | tf_op jit(solution)/shard_map/expert_weights/ppermute | solution.py:324
  0.0 28.7 %collective-permute-start.3 = (bf16[4096,384]{1,0:T(8,128)(2,1)}, bf16[4096,384]{1,0:T(8,128)(2,1)}, u32[]{:S(2)}, u32[]{:S(2)}) collective-permute-start(bf16[4096,384]{1,0:T(8,128)(2,1)} %bitcast.31), channel_id=1, source_target_pairs={{0,128},{128,0},{1,129},{129,1},{2,130},{130,2},{3,131},{131,3},{4... | collective-permute-start | bytes 9437192 | tf_op jit(solution)/shard_map/expert_weights/ppermute | solution.py:324
  0.5 28.2 %collective-permute-start.4 = (bf16[384,4096]{1,0:T(8,128)(2,1)}, bf16[384,4096]{1,0:T(8,128)(2,1)}, u32[]{:S(2)}, u32[]{:S(2)}) collective-permute-start(bf16[384,4096]{1,0:T(8,128)(2,1)} %bitcast.34), channel_id=1, source_target_pairs={{0,128},{128,0},{1,129},{129,1},{2,130},{130,2},{3,131},{131,3},{4... | collective-permute-start | bytes 9437192 | tf_op jit(solution)/shard_map/expert_weights/ppermute | solution.py:324
  2.5 26.2 %all-to-all-start = ((bf16[16,128,256]{2,1,0:T(8,128)(2,1)}), bf16[16,128,256]{2,1,0:T(8,128)(2,1)S(1)}, u32[]{:S(2)}, u32[]{:S(2)}) async-start(bf16[16,128,256]{2,1,0:T(8,128)(2,1)} %keys_values.1), calls=%async_computation | async-start | bytes 2097152 | tf_op jit(solution)/shard_map/keys_values/all_to_all | solution.py:280
  9.6 8.4 %collective-permute-start = (bf16[512,256]{1,0:T(8,128)(2,1)S(1)}, bf16[512,256]{1,0:T(8,128)(2,1)S(1)}, u32[]{:S(2)}, u32[]{:S(2)}) collective-permute-start(bf16[512,256]{1,0:T(8,128)(2,1)S(1)} %constant_dynamic-slice_fusion.refs_0_), channel_id=1, source_target_pairs={{0,1},{1,0},{2,3},{3,2},{4,5},{5,4},{6,7},{7,6},{8,9},{9,8},{10,11... | collective-permute-start | bytes 786440 | tf_op jit(solution)/shard_map/out_weight/ppermute | solution.py:329
  9.8 9.9 %collective-permute-start.1 = (bf16[512,256]{1,0:T(8,128)(2,1)S(1)}, bf16[512,256]{1,0:T(8,128)(2,1)S(1)}, u32[]{:S(2)}, u32[]{:S(2)}) collective-permute-start(bf16[512,256]{1,0:T(8,128)(2,1)S(1)} %constant_dynamic-slice_fusion.refs_0_), channel_id=1, source_target_pairs={{0,128},{128,0},{1,129},{129,1},{2,130},{130,2},{3,131},{131,3},{4... | collective-permute-start | bytes 786440 | tf_op jit(solution)/shard_map/out_weight/ppermute | solution.py:330
  18.1 19.7 %collective-permute-start.5 = (bf16[512,256]{1,0:T(8,128)(2,1)S(1)}, bf16[512,256]{1,0:T(8,128)(2,1)S(1)}, u32[]{:S(2)}, u32[]{:S(2)}) collective-permute-start(bf16[512,256]{1,0:T(8,128)(2,1)S(1)} %constant_dynamic-slice_fusion.refs_0_), channel_id=1, source_target_pairs={{0,8},{8,16},{16,24},{24,0},{1,9},{9,17},{17,25},{25,1},{2,10},{10... | collective-permute-start | bytes 786440 | tf_op jit(solution)/shard_map/out_weight/ppermute | solution.py:334
  19.7 18.1 %collective-permute-start.7 = (bf16[512,256]{1,0:T(8,128)(2,1)S(1)}, bf16[512,256]{1,0:T(8,128)(2,1)}, u32[]{:S(2)}, u32[]{:S(2)}) collective-permute-start(bf16[512,256]{1,0:T(8,128)(2,1)S(1)} %constant_dynamic-slice_fusion.refs_0_), channel_id=1, source_target_pairs={{0,24},{8,0},{16,8},{24,16},{1,25},{9,1},{17,9},{25,17},{2,26},{10... | collective-permute-start | bytes 786440 | tf_op jit(solution)/shard_map/out_weight/ppermute | solution.py:337
  28.7 9.1 %collective-permute-start.6 = (bf16[512,256]{1,0:T(8,128)(2,1)S(1)}, bf16[512,256]{1,0:T(8,128)(2,1)}, u32[]{:S(2)}, u32[]{:S(2)}) collective-permute-start(bf16[512,256]{1,0:T(8,128)(2,1)S(1)} %collective-permute-done.refs_1_), channel_id=1, source_target_pairs={{0,8},{8,16},{16,24},{24,0},{1,9},{9,17},{17,25},{25,1},{2,10},{10... | collective-permute-start | bytes 786440 | tf_op jit(solution)/shard_map/out_weight/ppermute | solution.py:336
  28.8 9.0 %collective-permute-start.8 = (bf16[512,256]{1,0:T(8,128)(2,1)S(1)}, bf16[512,256]{1,0:T(8,128)(2,1)}, u32[]{:S(2)}, u32[]{:S(2)}) collective-permute-start(bf16[512,256]{1,0:T(8,128)(2,1)S(1)} %collective-permute-done.refs_1_), channel_id=1, source_target_pairs={{0,24},{8,0},{16,8},{24,16},{1,25},{9,1},{17,9},{25,17},{2,26},{10... | collective-permute-start | bytes 786440 | tf_op jit(solution)/shard_map/out_weight/ppermute | solution.py:335
  32.0 5.8 %collective-permute-start.9 = (bf16[512,256]{1,0:T(8,128)(2,1)S(1)}, bf16[512,256]{1,0:T(8,128)(2,1)S(1)}, u32[]{:S(2)}, u32[]{:S(2)}) collective-permute-start(bf16[512,256]{1,0:T(8,128)(2,1)S(1)} %collective-permute-done.refs_1_), channel_id=1, source_target_pairs={{0,128},{128,0},{1,129},{129,1},{2,130},{130,2},{3,131},{131,3},{4... | collective-permute-start | bytes 786440 | tf_op jit(solution)/shard_map/out_weight/ppermute | solution.py:338
  37.9 18.8 %all-to-all-start.1 = ((bf16[8,64,1024]{2,1,0:T(8,128)(2,1)}), bf16[8,64,1024]{2,1,0:T(8,128)(2,1)S(1)}, u32[]{:S(2)}, u32[]{:S(2)}) async-start(bf16[8,64,1024]{2,1,0:T(8,128)(2,1)} %attention.1), calls=%async_computation.1 | async-start | bytes 2097152 | tf_op jit(solution)/shard_map/attention/all_to_all | solution.py:280
  41.9 9.5 %collective-permute-start.10 = (bf16[512,256]{1,0:T(8,128)(2,1)S(1)}, bf16[512,256]{1,0:T(8,128)(2,1)S(1)}, u32[]{:S(2)}, u32[]{:S(2)}) collective-permute-start(bf16[512,256]{1,0:T(8,128)(2,1)S(1)} %collective-permute-done.5.refs_2_), channel_id=1, source_target_pairs={{0,8},{8,16},{16,24},{24,0},{1,9},{9,17},{17,25},{25,1},{2,10},{10... | collective-permute-start | bytes 786440 | tf_op jit(solution)/shard_map/attention/ppermute | solution.py:361
  42.2 9.3 %collective-permute-start.11 = (bf16[512,256]{1,0:T(8,128)(2,1)}, bf16[512,256]{1,0:T(8,128)(2,1)S(1)}, u32[]{:S(2)}, u32[]{:S(2)}) collective-permute-start(bf16[512,256]{1,0:T(8,128)(2,1)} %collective-permute-done.8.refs_5_), channel_id=1, source_target_pairs={{0,24},{8,0},{16,8},{24,16},{1,25},{9,1},{17,9},{25,17},{2,26},{10... | collective-permute-start | bytes 786440 | tf_op jit(solution)/shard_map/attention/ppermute | solution.py:362
  45.2 6.8 %collective-permute-start.12 = (bf16[512,256]{1,0:T(8,128)(2,1)S(1)}, bf16[512,256]{1,0:T(8,128)(2,1)S(1)}, u32[]{:S(2)}, u32[]{:S(2)}) collective-permute-start(bf16[512,256]{1,0:T(8,128)(2,1)S(1)} %collective-permute-done.5.refs_2_), channel_id=1, source_target_pairs={{0,128},{128,0},{1,129},{129,1},{2,130},{130,2},{3,131},{131,3},{4... | collective-permute-start | bytes 786440 | tf_op jit(solution)/shard_map/attention/ppermute | solution.py:365
  45.2 8.0 %collective-permute-start.15 = (bf16[512,256]{1,0:T(8,128)(2,1)}, bf16[512,256]{1,0:T(8,128)(2,1)S(1)}, u32[]{:S(2)}, u32[]{:S(2)}) collective-permute-start(bf16[512,256]{1,0:T(8,128)(2,1)} %collective-permute-done.8.refs_5_), channel_id=1, source_target_pairs={{0,128},{128,0},{1,129},{129,1},{2,130},{130,2},{3,131},{131,3},{4... | collective-permute-start | bytes 786440 | tf_op jit(solution)/shard_map/attention/ppermute | solution.py:365
  45.7 6.4 %collective-permute-start.13 = (bf16[512,256]{1,0:T(8,128)(2,1)}, bf16[512,256]{1,0:T(8,128)(2,1)S(1)}, u32[]{:S(2)}, u32[]{:S(2)}) collective-permute-start(bf16[512,256]{1,0:T(8,128)(2,1)} %collective-permute-done.6.refs_3_), channel_id=1, source_target_pairs={{0,128},{128,0},{1,129},{129,1},{2,130},{130,2},{3,131},{131,3},{4... | collective-permute-start | bytes 786440 | tf_op jit(solution)/shard_map/attention/ppermute | solution.py:365
  51.4 1.9 collective-permute-start.16
  62.2 27.8 %all-to-all-start.2 = ((bf16[16,16,1024]{2,1,0:T(8,128)(2,1)}), bf16[16,16,1024]{2,1,0:T(8,128)(2,1)S(1)}, u32[]{:S(2)}, u32[]{:S(2)}) async-start(bf16[16,16,1024]{2,1,0:T(8,128)(2,1)} %projection.1), calls=%async_computation.2 | async-start | bytes 1048576 | tf_op jit(solution)/shard_map/projection/all_to_all | solution.py:280
  90.3 7.4 %collective-permute-start.19 = (bf16[16,4224]{1,0:T(8,128)(2,1)S(1)}, bf16[16,4224]{1,0:T(8,128)(2,1)S(1)}, u32[]{:S(2)}, u32[]{:S(2)}) collective-permute-start(bf16[16,4224]{1,0:T(8,128)(2,1)S(1)} %get-tuple-element.29.refs_0_), channel_id=1, source_target_pairs={{0,6},{2,0},{4,2},{6,4},{1,7},{3,1},{5,3},{7,5},{8,14},{10,8},{12,... | collective-permute-start | bytes 405512 | tf_op jit(solution)/shard_map/norm/ppermute | solution.py:403
  92.5 9.1 %collective-permute-start.18 = (bf16[16,4224]{1,0:T(8,128)(2,1)S(1)}, bf16[16,4224]{1,0:T(8,128)(2,1)S(1)}, u32[]{:S(2)}, u32[]{:S(2)}) collective-permute-start(bf16[16,4224]{1,0:T(8,128)(2,1)S(1)} %get-tuple-element.29.refs_0_), channel_id=1, source_target_pairs={{0,2},{2,4},{4,6},{6,0},{1,3},{3,5},{5,7},{7,1},{8,10},{10,12},{12... | collective-permute-start | bytes 405512 | tf_op jit(solution)/shard_map/norm/ppermute | solution.py:402
  97.7 10.3 %collective-permute-start.21 = (bf16[16,2176]{1,0:T(8,128)(2,1)S(1)}, bf16[16,2176]{1,0:T(8,128)(2,1)S(1)}, u32[]{:S(2)}, u32[]{:S(2)}) collective-permute-start(bf16[16,2176]{1,0:T(8,128)(2,1)S(1)} %slice.9), channel_id=1, source_target_pairs={{0,6},{2,0},{4,2},{6,4},{1,7},{3,1},{5,3},{7,5},{8,14},{10,8},{12,... | collective-permute-start | bytes 208904 | tf_op jit(solution)/shard_map/norm/ppermute | solution.py:407
  101.6 6.4 %collective-permute-start.20 = (bf16[16,2048]{1,0:T(8,128)(2,1)S(1)}, bf16[16,2048]{1,0:T(8,128)(2,1)S(1)}, u32[]{:S(2)}, u32[]{:S(2)}) collective-permute-start(bf16[16,2048]{1,0:T(8,128)(2,1)S(1)} %slice.8), channel_id=1, source_target_pairs={{0,2},{2,4},{4,6},{6,0},{1,3},{3,5},{5,7},{7,1},{8,10},{10,12},{12... | collective-permute-start | bytes 196616 | tf_op jit(solution)/shard_map/norm/ppermute | solution.py:406
  148.6 29.8 %all-to-all-start.4 = ((bf16[32,8,4096]{2,1,0:T(8,128)(2,1)}), bf16[32,8,4096]{2,1,0:T(8,128)(2,1)S(1)}, u32[]{:S(2)}, u32[]{:S(2)}) async-start(bf16[32,8,4096]{2,1,0:T(8,128)(2,1)} %bitcast.19), calls=%async_computation.4 | async-start | bytes 4194304 | tf_op jit(solution)/shard_map/experts/all_to_all | solution.py:280
  (18 other events, 310.3 us)
